TPU v7x, 32 devices: a whole 2x2x4 slice. The times are simulated.
32 devices in a mesh: blk: 16 (over z, y, core), rep: 2 (over x).
Axes of the slice: x: 2, y: 2, z: 4, core: 2. Of those that a mesh axis runs over, the one named last changes fastest.
Arguments:
- pooled: bfloat16 [2, 2048, 1536], P('rep', 'blk'), may hold values from -6 to 6
- w_img: bfloat16 [1536, 1024], replicated, may hold values from -0.15625 to 0.15625
- text_emb: bfloat16 [2, 2048, 1024], P('rep', 'blk'), may hold values from -6 to 6
- pos_index: int32 [2, 2048], P('rep', 'blk'), may hold values from 0 to 2047, each once within a row
- log_scale: float32 [1], replicated, may hold values from 1.5 to 2.5
- bias: float32 [1], replicated, may hold values from -2 to -0.5
Outputs:
- row_loss: float32 [2, 2048], P('rep', 'blk')
- weight_grad: float32 [1536, 1024], P(('blk', 'rep'))
- text_grad: float32 [2, 2048, 1024], P('rep', 'blk')
Inputs may be any that keep to these rules, and one draw needn't show every extreme that they name: `pos_index`: each group's row is a permutation of 0 to 2047.
All inputs are finite; a program needn't handle non-finite values.
Results may differ from a plain program's by a relative error of at most 0.0052.
Values may be sent and summed in bfloat16 or wider, within the bound.
A program may use at most 192 MiB of HBM per device.

v0:
```python
import jax
import jax.numpy as jnp
from jax import lax
from jax.sharding import PartitionSpec as P


def normalize(rows):
    squares = jnp.sum(rows * rows, axis=-1, keepdims=True)
    inverse = lax.rsqrt(squares + 1e-06)
    return (rows * inverse, inverse)


def pair_terms(left, right, left_pos, right_start, scale_value, shift):
    logits = scale_value * jnp.dot(left, right.T, preferred_element_type=jnp.float32) + shift
    columns = right_start + jnp.arange(right.shape[0], dtype=jnp.int32)
    sign = jnp.where(left_pos[:, None] == columns[None, :], 1.0, -1.0).astype(jnp.float32)
    losses = jax.nn.softplus(-sign * logits)
    coeffs = (-sign * jax.nn.sigmoid(-sign * logits) * scale_value).astype(jnp.bfloat16)
    return (jnp.sum(losses, axis=1), coeffs)


def transpose_dot(coeffs, rows):
    return lax.dot_general(
        coeffs, rows, (((0,), (0,)), ((), ())), preferred_element_type=jnp.float32
    )


def shards(pooled, w_img, text_emb, pos_index, log_scale, bias):
    scale_value = jnp.exp(log_scale[0])
    shift = bias[0]
    features = pooled[0]
    my_pos = pos_index[0]
    row_count = features.shape[0]
    group_size = row_count * lax.axis_size("blk")
    my_start = lax.axis_index("blk") * row_count
    projected = jnp.dot(features, w_img, preferred_element_type=jnp.float32)
    image_unit, image_inv = normalize(projected)
    image_low = image_unit.astype(jnp.bfloat16)
    text_unit, text_inv = normalize(text_emb[0].astype(jnp.float32))
    text_low = text_unit.astype(jnp.bfloat16)
    piece = lax.all_gather(text_low, "blk", axis=0, tiled=True)
    row_sums, coeffs = pair_terms(image_low, piece, my_pos, jnp.int32(0), scale_value, shift)
    loss_total = row_sums
    image_dir = jnp.dot(coeffs, piece, preferred_element_type=jnp.float32)
    pieces = (
        lax.all_gather(image_low, "blk", axis=0, tiled=True),
        lax.all_gather(my_pos, "blk", axis=0, tiled=True),
    )
    row_sums, coeffs = pair_terms(pieces[0], text_low, pieces[1], my_start, scale_value, shift)
    text_dir = transpose_dot(coeffs, pieces[0])
    image_back = (
        (image_dir - image_unit * jnp.sum(image_unit * image_dir, axis=-1, keepdims=True))
        * image_inv
    ).astype(jnp.bfloat16)
    text_back = (
        text_dir - text_unit * jnp.sum(text_unit * text_dir, axis=-1, keepdims=True)
    ) * text_inv
    weight_part = transpose_dot(features, image_back)
    weight_sum = lax.psum_scatter(weight_part, ("blk", "rep"), scatter_dimension=0, tiled=True)
    return ((loss_total / group_size)[None], weight_sum / 64.0, text_back[None])


def solution(mesh):
    return jax.shard_map(
        shards,
        mesh=mesh,
        in_specs=(P("rep", "blk", None), P(), P("rep", "blk", None), P("rep", "blk"), P(), P()),
        out_specs=(P("rep", "blk"), P(("blk", "rep"), None), P("rep", "blk", None)),
        check_vma=False,
    )
```

profile of v0, /device:TPU:0, one launch (start us, length us, event | category | flops | bytes accessed | tf_op | source)
XLA Modules:
  0.0 246.1 jit_solution(710342724317929108)
XLA Ops:
  7.2 0.0 copy-start
  7.2 0.0 copy-start.5
  7.2 0.0 all-gather.4.cloned.1.call-start
  7.2 1.2 fusion.21
  8.5 1.8 fusion.15
  10.2 0.0 all-gather.4.cloned.1.call-update
  10.3 0.0 all-gather.6.cloned.1.call-start
  10.3 0.0 copy-done
  10.3 1.7 multiply_reduce_fusion.1
  12.0 0.0 copy-start.1
  12.0 0.8 copy-done.1
  12.8 0.8 multiply_convert_fusion.3
  13.6 0.0 all-gather.6.cloned.1.call-update
  13.6 0.0 reduce-scatter.4.cloned.1.call-start
  15.0 48.7 %all-gather.4.cloned.1.call-done = bf16[2048,1024]{1,0:T(8,128)(2,1)} async-done(((bf16[128,1024]{1,0:T(8,128)(2,1)}), bf16[2048,1024]{1,0:T(8,128)(2,1)}) %all-gather.4.cloned.1.call-update) | async-done | bytes 4194320 | tf_op jit(solution)/shard_map/all_gather | solution.py:41
  63.7 0.0 copy-start.2
  63.7 0.0 copy-start.6
  63.7 0.0 copy-done.5
  63.7 4.6 %fusion.11 = (f32[128]{0:T(128)S(1)}, f32[128,2048]{1,0:T(8,128)S(1)}) fusion(f32[]{:T(128)} %bitcast.32, bf16[128,1024]{1,0:T(8,128)(2,1)} %multiply_convert_fusion.3, bf16[2048,1024]{1,0:T(8,128)(2,1)} %all-gather.4.cloned.1.call-done, f32[]{:T(128)} %bitcast.1, s32[128]{0:T(128)S(1)} %bitcast.35), kind=kOutput, calls=%fused_computation.15 | convolution fusion | flops 540278656 | bytes 5506056 | tf_op jit(solution)/shard_map/dot_general | solution.py:14
  68.2 0.0 copy-done.2
  68.2 0.0 copy-done.6
  68.3 0.0 copy-start.4
  68.3 1.0 multiply_reduce_fusion
  69.3 0.0 copy-done.4
  69.3 3.8 %convolution_bitcast_fusion = f32[1536,1024]{0,1:T(8,128)} fusion(bf16[1,128,1536]{2,1,0:T(8,128)(2,1)S(1)} %copy-done.4, f32[128,1024]{1,0:T(8,128)S(1)} %get-tuple-element.14, f32[128,1024]{1,0:T(8,128)S(1)} %copy-done.2, f32[128]{0:T(128)S(1)} %get-tuple-element.13, f32[128]{0:T(128)S(1)} %add_rsqrt_fusion.1), kind=kOutput, calls=%fused_computation | convolution fusion | flops 403308544 | bytes 7734272 | tf_op jit(solution)/shard_map/dot_general | solution.py:23
  73.1 6.6 %copy.11 = f32[1536,1024]{1,0:T(8,128)} copy(f32[1536,1024]{0,1:T(8,128)} %convolution_bitcast_fusion) | data formatting | bytes 12582912
  79.7 0.0 copy-start.3
  79.7 0.0 reduce-scatter.4.cloned.1.call-update
  79.7 19.0 %all-gather = s32[1,2048]{1,0:T(1,128)S(1)} all-gather(s32[1,128]{1,0:T(1,128)S(1)} %copy-done.5), channel_id=2, replica_groups=mesh['blk'=16,'rep'=2] {'blk'}, dimensions={1}, use_global_device_ids=true | all-gather | bytes 8704 | tf_op jit(solution)/shard_map/all_gather | solution.py:47
  98.7 0.5 multiply_bitcast_fusion
  99.2 15.8 %all-gather.6.cloned.1.call-done = bf16[2048,1024]{1,0:T(8,128)(2,1)} async-done(((bf16[128,1024]{1,0:T(8,128)(2,1)}), bf16[2048,1024]{1,0:T(8,128)(2,1)}) %all-gather.6.cloned.1.call-update) | async-done | bytes 4194320 | tf_op jit(solution)/shard_map/all_gather | solution.py:46
  115.1 0.0 copy-done.3
  115.1 7.0 %fusion.17 = (f32[128]{0:T(128)S(1)}, f32[128,1024]{1,0:T(8,128)}) fusion(bf16[1,128,1024]{2,1,0:T(8,128)(2,1)S(1)} %copy-done.3, f32[128]{0:T(128)S(1)} %add_rsqrt_fusion, bf16[2048,1024]{1,0:T(8,128)(2,1)} %all-gather.6.cloned.1.call-done, f32[]{:T(128)} %bitcast.33, f32[]{:T(128)} %bitcast.1, s32[128]{0:T(128)S(1)} %iota_add_fusion, s32[2048]{0:T(1024)S(1)} %bitcast.34), kind=kOutput, calls=%fused_computation.26 | convolution fusion | flops 1077804928 | bytes 4990472 | tf_op jit(solution)/shard_map/dot_general | solution.py:23
  122.1 2.1 fusion.20
  124.2 109.7 %reduce-scatter.4.cloned.1.call-done = f32[48,1024]{1,0:T(8,128)} async-done(((f32[1536,1024]{1,0:T(8,128)}), f32[48,1024]{1,0:T(8,128)}) %reduce-scatter.4.cloned.1.call-update) | async-done | bytes 196624
  233.9 1.9 copy.12
  235.8 1.9 broadcast_multiply_fusion
  237.7 1.9 copy.10
  (3 shorter events, 0.0 us)
Async XLA Ops:
  7.2 3.1 %copy-start = (bf16[1536,1024]{1,0:T(8,128)(2,1)S(1)}, bf16[1536,1024]{1,0:T(8,128)(2,1)}, u32[]{:S(2)}) copy-start(bf16[1536,1024]{1,0:T(8,128)(2,1)} %param.7) | copy-start | bytes 9437188
  7.2 56.5 %copy-start.5 = (s32[1,128]{1,0:T(1,128)S(1)}, s32[1,128]{1,0:T(1,128)}, u32[]{:S(2)}) copy-start(s32[1,128]{1,0:T(1,128)} %param.9) | copy-start | bytes 1540
  7.2 56.5 %all-gather.4.cloned.1.call-start = ((), (), s32[]{:S(2)}) async-start(), calls=%async_computation.1 | async-start | bytes 4456448 | tf_op jit(solution)/shard_map/all_gather | solution.py:41
  10.3 104.8 %all-gather.6.cloned.1.call-start = ((), (), s32[]{:S(2)}) async-start(), calls=%async_computation.2 | async-start | bytes 4456448 | tf_op jit(solution)/shard_map/all_gather | solution.py:46
  12.0 0.8 copy-start.1
  13.6 220.3 %reduce-scatter.4.cloned.1.call-start = ((), (), s32[]{:S(2)}) async-start(), calls=%async_computation.3 | async-start | bytes 6488064
  63.7 4.6 %copy-start.2 = (f32[128,1024]{1,0:T(8,128)S(1)}, f32[128,1024]{1,0:T(8,128)}, u32[]{:S(2)}) copy-start(f32[128,1024]{1,0:T(8,128)} %copy-done.1) | copy-start | bytes 1572868
  63.7 4.6 %copy-start.6 = (bf16[2048,1024]{1,0:T(8,128)(2,1)S(1)}, bf16[2048,1024]{1,0:T(8,128)(2,1)}, u32[]{:S(2)}) copy-start(bf16[2048,1024]{1,0:T(8,128)(2,1)} %all-gather.4.cloned.1.call-done) | copy-start | bytes 12582916
  68.3 1.1 copy-start.4
  79.7 35.4 %copy-start.3 = (bf16[1,128,1024]{2,1,0:T(8,128)(2,1)S(1)}, bf16[1,128,1024]{2,1,0:T(8,128)(2,1)}, u32[]{:S(2)}) copy-start(bf16[1,128,1024]{2,1,0:T(8,128)(2,1)} %param.8) | copy-start | bytes 786436
Sparse Core Ops, SparseCore 0:
  10.4 53.2 all-gather.3
  65.8 49.2 all-gather.5
  120.7 113.1 reduce-scatter.3
where the time goes:
time: 247 us; the launch traced here: 246 us
  waiting for transfers between devices  174 us (70%)
  blocking collectives  19 us (8%)
  matrix products  18.1 us (7%)
  between operations  15.2 us (6%)
  local copies, waits for them, and re-layouts  11.2 us (5%)
  other arithmetic  8.24 us (3%)
    unnamed x4, waiting for transfers between devices  110 us
    all_gather x1, waiting for transfers between devices, shards(): piece = lax.all_gather(text_low, 'blk', axis=0, tiled=True)  48.7 us
    all_gather x1, blocking collectives, shards(): lax.all_gather(my_pos, 'blk', axis=0, tiled=True)  19 us
    all_gather x1, waiting for transfers between devices, shards(): lax.all_gather(image_low, 'blk', axis=0, tiled=True)  15.8 us
    unnamed x17, local copies, waits for them, and re-layouts  11.2 us
    dot_general x2, matrix products, transpose_dot(): lax.dot_general(coeffs, rows, (((0,), (0,)), ((), ())), preferred_element...  10.8 us
  transfers between devices with their start and end apart: 3, of which 3 were waited for; matrix products, arithmetic and copies ran while one was open for 11% of the time, Pallas kernels for 0%

commit v1 on v0

--- a/solution.py
+++ b/solution.py
@@ -1,7 +1,360 @@
 import jax
 import jax.numpy as jnp
 from jax import lax
+from jax.experimental import pallas as pl
+from jax.experimental.pallas import tpu as pltpu
 from jax.sharding import PartitionSpec as P
+
+F32 = jnp.float32
+BF16 = jnp.bfloat16
+LINE = 4
+QUAD = 4
+LAYER = 8
+
+
+def fused_kernel(
+    pooled, w_hbm, text_in, pos_in, log_scale, bias,
+    loss_out, weight_out, text_out,
+    w, text_all, image_all, pos_all, pt_send, pt_all,
+    text_unit, image_unit, td_own, td_send, td_recv, id_acc, id_send, id_recv, id_far, id_far_recv,
+    loss_part, loss_recv, ib_all, weight_own, wp_send, wp_recv,
+    w_sem, tg_s, tg_f, tg_r, ig_s, ig_r, pg_s, pg_r, pt_s, pt_r, td_s, td_r,
+    id_s, id_r, ls_s, ls_r, ib_s, ib_f, ib_r, wp_s, wp_r,
+):
+    blk, x = lax.axis_index("blk"), lax.axis_index("rep")
+    z, y, c = blk // 4, (blk // 2) % 2, blk % 2
+    rows, emb = text_in.shape
+    oy, oc, ox = 1 - y, 1 - c, 1 - x
+
+    def dev(zz, yy, cc, xx):
+        return {"blk": zz * 4 + yy * 2 + cc, "rep": xx}
+
+    def layer_of(yy, cc, xx):
+        return yy * 4 + cc * 2 + xx
+
+    def layer_dev(j):
+        return dev(z, j // 4, (j // 2) % 2, j % 2)
+
+    def remote(src, dst, send, recv, device):
+        return pltpu.make_async_remote_copy(
+            src_ref=src, dst_ref=dst, send_sem=send, recv_sem=recv,
+            device_id=device, device_id_type=pl.DeviceIdType.MESH,
+        )
+
+    q, me = y * 2 + c, layer_of(y, c, x)
+    far = z // 2
+    mid = z * (1 - far) + (LINE - 1 - z) * far
+
+    def flip(base):
+        return base + far * (LINE - 1 - 2 * base)
+
+    order = [flip(mid), flip(1 - mid), flip(2), flip(3)]
+
+    w_copy = pltpu.make_async_copy(w_hbm, w, w_sem)
+    w_copy.start()
+    barrier = pltpu.get_barrier_semaphore()
+    for k in range(1, LAYER):
+        pl.semaphore_signal(barrier, inc=1, device_id=layer_dev((me + k) % LAYER), device_id_type=pl.DeviceIdType.MESH)
+    for k in range(1, LINE):
+        pl.semaphore_signal(
+            barrier, inc=1, device_id=dev((z + k) % LINE, y, c, x), device_id_type=pl.DeviceIdType.MESH
+        )
+
+    raw = text_in[...].astype(F32)
+    text_inv = lax.rsqrt(jnp.sum(raw * raw, axis=-1, keepdims=True) + 1e-06)
+    unit = raw * text_inv
+    text_unit[...] = unit
+    text_all[z] = unit.astype(BF16)
+    pos_all[q] = pos_in[...]
+    pl.semaphore_wait(barrier, LAYER - 1 + LINE - 1)
+
+    own_a = remote(text_all.at[z], text_all.at[z], tg_s.at[0], tg_r.at[z], dev(flip(1 + mid), y, c, x))
+    own_b = remote(text_all.at[z], text_all.at[z], tg_s.at[1], tg_r.at[z], dev(flip(0), y, c, x))
+    own_a.start()
+
+    @pl.when(mid == 1)
+    def _():
+        own_b.start()
+
+    peers = [(y, oc), (oy, c), (oy, oc)]
+    pos_copies = [
+        remote(pos_all.at[q], pos_all.at[q], pg_s.at[k], pg_r.at[q], dev(z, yy, cc, x))
+        for k, (yy, cc) in enumerate(peers)
+    ]
+    for copy in pos_copies:
+        copy.start()
+
+    w_copy.wait()
+    projected = jnp.dot(pooled[...], w[...], preferred_element_type=F32)
+    image_inv = lax.rsqrt(jnp.sum(projected * projected, axis=-1, keepdims=True) + 1e-06)
+    unit = projected * image_inv
+    image_unit[...] = unit
+    image_all[q] = unit.astype(BF16)
+    image_copies = [
+        remote(image_all.at[q], image_all.at[q], ig_s.at[k], ig_r.at[q], dev(z, yy, cc, x))
+        for k, (yy, cc) in enumerate(peers[:2])
+    ]
+    image_copies[1].start()
+    image_copies[0].start()
+
+    turned = pooled[...].T.reshape(LINE, LAYER, -1, rows)
+    for j in range(LAYER):
+        for t in range(LINE):
+            pt_send[j, t] = turned[t, j]
+    pt_all[me] = pt_send[me]
+
+    def pt_copy(k):
+        j = (me + k) % LAYER
+        return remote(pt_send.at[j], pt_all.at[me], pt_s.at[j], pt_r.at[me], layer_dev(j))
+
+    for k in range(1, LAYER):
+        pt_copy(k).start()
+
+    def forward(i):
+        s = order[i]
+        slot = text_all.at[s]
+        return remote(slot, slot, tg_f.at[i], tg_r.at[s], dev(flip(2 if i == 1 else 0), y, c, x))
+
+    def arrive(i):
+        copy = forward(i)
+        copy.wait_recv()
+
+        @pl.when(mid == 1)
+        def _():
+            copy.start()
+
+    arrive(1)
+
+    @pl.when(mid == 1)
+    def _():
+        copy = forward(2)
+        copy.wait_recv()
+        copy.start()
+
+    for k, (yy, cc) in enumerate(peers):
+        qq = yy * 2 + cc
+        remote(pos_all.at[qq], pos_all.at[qq], pg_s.at[k], pg_r.at[qq], dev(z, yy, cc, x)).wait_recv()
+
+    def image_slot(k, yy, cc):
+        slot = image_all.at[yy * 2 + cc]
+        return remote(slot, slot, ig_s.at[k], ig_r.at[yy * 2 + cc], dev(z, y, oc, x))
+
+    image_pass = image_slot(2, oy, c)
+    image_pass.wait_recv()
+    image_pass.start()
+    image_slot(0, y, oc).wait_recv()
+    image_slot(0, oy, oc).wait_recv()
+
+    images = image_all[...].reshape(QUAD * rows, emb)
+    pos = jnp.concatenate([pos_all[k] for k in range(QUAD)], axis=1)
+    scale = jnp.exp(jnp.full((1, QUAD * rows), log_scale[0], F32))
+    shift = bias[0]
+    losses = jnp.zeros((1, QUAD * rows), F32)
+
+    def text_dir_copy(i):
+        s = order[i]
+        return remote(td_send.at[s], td_recv.at[z], td_s.at[s], td_r.at[z], dev(s, y, c, x))
+
+    for i in range(LINE):
+        if i == 2:
+
+            @pl.when(mid == 0)
+            def _():
+                forward(2).wait_recv()
+
+        if i == 3:
+            arrive(3)
+        s = order[i]
+        text = text_all[s]
+        dots = lax.dot_general(text, images, (((1,), (1,)), ((), ())), preferred_element_type=F32)
+        logits = scale * dots + shift
+        owner = (s * QUAD + q) * rows + lax.broadcasted_iota(jnp.int32, (rows, QUAD * rows), 0)
+        sign = jnp.where(owner == pos, 1.0, -1.0).astype(F32)
+        value = -sign * logits
+        losses += jnp.sum(
+            jnp.maximum(value, 0.0) + jnp.log1p(jnp.exp(-jnp.abs(value))), axis=0, keepdims=True
+        )
+        coeffs = (-sign * jax.nn.sigmoid(value) * scale).astype(BF16)
+        text_part = jnp.dot(coeffs, images, preferred_element_type=F32)
+        if i == 0:
+            td_own[...] = text_part
+        else:
+            td_send[s] = text_part.astype(BF16)
+            text_dir_copy(i).start()
+        image_part = lax.dot_general(
+            coeffs, text, (((0,), (0,)), ((), ())), preferred_element_type=F32
+        ).reshape(QUAD, rows, emb)
+        if i == 0:
+            id_acc[...] = image_part
+        else:
+            id_acc[...] += image_part
+
+    id_send[1] = id_acc[oy * 2 + oc].astype(BF16)
+    pair = dev(z, y, oc, x)
+    id_copies = [remote(id_send.at[k], id_recv.at[k], id_s.at[k], id_r.at[k], pair) for k in range(2)]
+    id_copies[1].start()
+    id_send[0] = id_acc[y * 2 + oc].astype(BF16)
+    id_copies[0].start()
+    for k in range(QUAD):
+        loss_part[k] = losses[:, k * rows : (k + 1) * rows]
+    loss_copies = [
+        remote(loss_part.at[yy * 2 + cc], loss_recv.at[q], ls_s.at[k], ls_r.at[q], dev(z, yy, cc, x))
+        for k, (yy, cc) in enumerate(peers)
+    ]
+    for copy in loss_copies:
+        copy.start()
+    id_copies[1].wait_recv()
+    id_far[...] = (id_acc[oy * 2 + c] + id_recv[1].astype(F32)).astype(BF16)
+    far_copy = remote(id_far, id_far_recv, id_s.at[2], id_r.at[2], dev(z, oy, c, x))
+    far_copy.start()
+    id_copies[0].wait_recv()
+    near = id_acc[q] + id_recv[0].astype(F32)
+    far_copy.wait_recv()
+    image_dir = near + id_far_recv[...].astype(F32)
+    unit = image_unit[...]
+    ib_all[me] = (
+        (image_dir - unit * jnp.sum(unit * image_dir, axis=-1, keepdims=True)) * image_inv
+    ).astype(BF16)
+
+    others = [(oy, c, ox), (oy, c, x), (y, c, ox), (y, oc, x)]
+    ib_copies = [
+        remote(ib_all.at[me], ib_all.at[me], ib_s.at[k], ib_r.at[me], dev(z, *other))
+        for k, other in enumerate(others)
+    ]
+    for copy in ib_copies:
+        copy.start()
+
+    def ib_slot(k, *other):
+        slot = ib_all.at[layer_of(*other)]
+        return remote(slot, slot, ib_f.at[k], ib_r.at[layer_of(*other)], pair)
+
+    ib_passes = [ib_slot(k, *other) for k, other in enumerate([(oy, c, x), (y, c, ox), (oy, c, ox)])]
+    for copy in ib_passes:
+        copy.wait_recv()
+        copy.start()
+    for other in [(y, oc, x), (oy, oc, x), (y, oc, ox), (oy, oc, ox)]:
+        ib_slot(0, *other).wait_recv()
+
+    def pt_recv(k):
+        j = (me + k) % LAYER
+        return remote(pt_all.at[j], pt_all.at[j], pt_s.at[j], pt_r.at[j], layer_dev(j))
+
+    for k in range(1, LAYER):
+        pt_recv(k).wait_recv()
+
+    share = pt_all.shape[2]
+    turned_all = jnp.concatenate([pt_all[j].reshape(LINE * share, rows) for j in range(LAYER)], axis=1)
+    weight_part = jnp.dot(turned_all, ib_all[...].reshape(LAYER * rows, emb), preferred_element_type=F32)
+    for t in range(LINE):
+        weight_own[t] = weight_part[t * share : (t + 1) * share]
+        wp_send[t] = weight_part[t * share : (t + 1) * share].astype(BF16)
+
+    def weight_copy(k):
+        t = (z + k) % LINE
+        return remote(wp_send.at[t], wp_recv.at[z], wp_s.at[t], wp_r.at[z], dev(t, y, c, x))
+
+    def from_line(recv, sem, k):
+        t = (z + k) % LINE
+        return remote(recv.at[t], recv.at[t], wp_s.at[t], sem.at[t], dev(t, y, c, x))
+
+    for k in range(1, LINE):
+        weight_copy(k).start()
+
+    total = td_own[...]
+    for k in range(1, LINE):
+        from_line(td_recv, td_r, k).wait_recv()
+        total += td_recv[(z + k) % LINE].astype(F32)
+    unit = text_unit[...]
+    text_out[...] = (total - unit * jnp.sum(unit * total, axis=-1, keepdims=True)) * text_inv
+
+    total = loss_part[q]
+    for k, (yy, cc) in enumerate(peers):
+        qq = yy * 2 + cc
+        remote(loss_recv.at[qq], loss_recv.at[qq], ls_s.at[k], ls_r.at[qq], dev(z, yy, cc, x)).wait_recv()
+        total += loss_recv[qq]
+    loss_out[...] = total / (LINE * QUAD * rows)
+
+    total = weight_own[z]
+    for k in range(1, LINE):
+        from_line(wp_recv, wp_r, k).wait_recv()
+        total += wp_recv[(z + k) % LINE].astype(F32)
+    weight_out[...] = total / 64.0
+
+    own_a.wait_send()
+
+    @pl.when(mid == 1)
+    def _():
+        own_b.wait_send()
+        for i in range(1, LINE):
+            forward(i).wait_send()
+
+    for copy in pos_copies + image_copies + [image_pass] + id_copies + [far_copy] + loss_copies:
+        copy.wait_send()
+    for copy in ib_copies + ib_passes:
+        copy.wait_send()
+    for k in range(1, LAYER):
+        pt_copy(k).wait_send()
+    for k in range(1, LINE):
+        text_dir_copy(k).wait_send()
+        weight_copy(k).wait_send()
+
+
+def fused(pooled, w_img, text_emb, pos_index, log_scale, bias):
+    _, rows, width = pooled.shape
+    emb = w_img.shape[1]
+    share = width // (LINE * LAYER)
+    vmem, dma = pltpu.VMEM, pltpu.SemaphoreType.DMA
+    in_vmem = pl.BlockSpec(memory_space=pltpu.VMEM)
+    in_smem = pl.BlockSpec(memory_space=pltpu.SMEM)
+    block = (rows, emb)
+    loss, weight, text = pl.pallas_call(
+        fused_kernel,
+        out_shape=(
+            jax.ShapeDtypeStruct((1, rows), F32),
+            jax.ShapeDtypeStruct((share, emb), F32),
+            jax.ShapeDtypeStruct(block, F32),
+        ),
+        in_specs=[in_vmem, pl.BlockSpec(memory_space=pl.ANY), in_vmem, in_vmem, in_smem, in_smem],
+        out_specs=(in_vmem, in_vmem, in_vmem),
+        scratch_shapes=[
+            vmem((width, emb), BF16),
+            vmem((LINE,) + block, BF16),
+            vmem((QUAD,) + block, BF16),
+            vmem((QUAD, 1, rows), jnp.int32),
+            vmem((LAYER, LINE, share, rows), BF16),
+            vmem((LAYER, LINE, share, rows), BF16),
+            vmem(block, F32),
+            vmem(block, F32),
+            vmem(block, F32),
+            vmem((LINE,) + block, BF16),
+            vmem((LINE,) + block, BF16),
+            vmem((QUAD,) + block, F32),
+            vmem((2,) + block, BF16),
+            vmem((2,) + block, BF16),
+            vmem(block, BF16),
+            vmem(block, BF16),
+            vmem((QUAD, 1, rows), F32),
+            vmem((QUAD, 1, rows), F32),
+            vmem((LAYER,) + block, BF16),
+            vmem((LINE, share, emb), F32),
+            vmem((LINE, share, emb), BF16),
+            vmem((LINE, share, emb), BF16),
+            dma,
+            dma((2,)), dma((LINE,)), dma((LINE,)),
+            dma((3,)), dma((QUAD,)),
+            dma((3,)), dma((QUAD,)),
+            dma((LAYER,)), dma((LAYER,)),
+            dma((LINE,)), dma((LINE,)),
+            dma((3,)), dma((3,)),
+            dma((3,)), dma((QUAD,)),
+            dma((4,)), dma((3,)), dma((LAYER,)),
+            dma((LINE,)), dma((LINE,)),
+        ],
+        compiler_params=pltpu.CompilerParams(
+            collective_id=0, has_side_effects=True, vmem_limit_bytes=48 * 2**20
+        ),
+    )(pooled[0], w_img, text_emb[0], pos_index, log_scale, bias)
+    return loss, weight, text[None]
 
 
 def normalize(rows):
@@ -25,7 +378,7 @@
     )
 
 
-def shards(pooled, w_img, text_emb, pos_index, log_scale, bias):
+def plain(pooled, w_img, text_emb, pos_index, log_scale, bias):
     scale_value = jnp.exp(log_scale[0])
     shift = bias[0]
     features = pooled[0]
@@ -61,6 +414,12 @@
 
 
 def solution(mesh):
+    def shards(pooled, w_img, text_emb, pos_index, log_scale, bias):
+        _, rows, width = pooled.shape
+        fits = mesh.shape["blk"] == LINE * QUAD and mesh.shape["rep"] * QUAD == LAYER
+        fits = fits and rows % 128 == 0 and width % (LINE * LAYER * 16) == 0
+        return (fused if fits else plain)(pooled, w_img, text_emb, pos_index, log_scale, bias)
+
     return jax.shard_map(
         shards,
         mesh=mesh,

time: 247 us -> 72.5 us (0.29)
  waiting for transfers between devices: 174 us -> 0 us
  Pallas kernels: 0 us -> 63.8 us
  blocking collectives: 19 us -> 0 us
  matrix products: 18.1 us -> 0 us
  between operations: 15.2 us -> 1.94 us
  other arithmetic: 8.24 us -> 0 us
  local copies, waits for them, and re-layouts: 11.2 us -> 6.46 us
    unnamed x4 -> x0, waiting for transfers between devices: 110 us -> none
    all_gather x2 -> x0, waiting for transfers between devices: 64.5 us -> none  [the longest x1 48.7 us: shards(): piece = lax.all_gather(text_low, 'blk', axis=0, tiled=True)]
    pallas_call x0 -> x1, Pallas kernels: none -> 63.8 us  [fused(): pl.pallas_call(fused_kernel, out_shape=(jax.ShapeDtypeStruct((1, rows), F...]
    all_gather x1 -> x0, blocking collectives: 19 us -> none  [shards(): lax.all_gather(my_pos, 'blk', axis=0, tiled=True)]
    dot_general x5 -> x0, matrix products: 18.1 us -> none  [the longest x2 10.8 us: transpose_dot(): lax.dot_general(coeffs, rows, (((0,), (0,)), ((), ())), preferred_element...]
    unnamed x17 -> x11, local copies, waits for them, and re-layouts: 11.2 us -> 6.46 us
    convert_element_type x2 -> x0, other arithmetic: 2.55 us -> none  [the longest x1 1.76 us: shards(): text_low = text_unit.astype(jnp.bfloat16)]
  transfers between devices with their start and end apart: 3 -> 0, of which waited for: 3 -> 0; matrix products, arithmetic and copies ran while one was open for 11% -> 0% of each run, Pallas kernels for 0% -> 0%
where the time goes in v1:
time: 72.5 us; the launch traced here: 72.2 us
  Pallas kernels  63.8 us (88%)
  local copies, waits for them, and re-layouts  6.46 us (9%)
  between operations  1.94 us (3%)
    pallas_call x1, Pallas kernels, fused(): pl.pallas_call(fused_kernel, out_shape=(jax.ShapeDtypeStruct((1, rows), F...  63.8 us
    unnamed x11, local copies, waits for them, and re-layouts  6.46 us

profile of v1, /device:TPU:0, one launch (start us, length us, event | category | flops | bytes accessed | tf_op | source)
XLA Modules:
  0.0 72.2 jit_solution(3833124867690596430)
XLA Ops:
  1.9 0.0 copy-start
  1.9 1.9 %copy-done = bf16[1536,1024]{1,0:T(8,128)(2,1)S(1)} copy-done((bf16[1536,1024]{1,0:T(8,128)(2,1)S(1)}, bf16[1536,1024]{1,0:T(8,128)(2,1)}, u32[]{:S(2)}) %copy-start) | copy-done | bytes 3145752
  3.8 0.0 copy-start.1
  3.8 1.0 %copy-done.1 = bf16[1,128,1536]{2,1,0:T(8,128)(2,1)S(1)} copy-done((bf16[1,128,1536]{2,1,0:T(8,128)(2,1)S(1)}, bf16[1,128,1536]{2,1,0:T(8,128)(2,1)}, u32[]{:S(2)}) %copy-start.1) | copy-done | bytes 393240
  4.8 0.0 copy-start.2
  4.8 0.9 %copy-done.2 = bf16[1,128,1024]{2,1,0:T(8,128)(2,1)S(1)} copy-done((bf16[1,128,1024]{2,1,0:T(8,128)(2,1)S(1)}, bf16[1,128,1024]{2,1,0:T(8,128)(2,1)}, u32[]{:S(2)}) %copy-start.2) | copy-done | bytes 262168
  5.8 0.0 copy-start.3
  5.8 0.7 copy-done.3
  6.4 63.8 %shard_map.85 = (f32[1,128]{1,0:T(1,128)S(1)}, f32[48,1024]{1,0:T(8,128)S(1)}, f32[128,1024]{1,0:T(8,128)S(1)}) custom-call(bf16[128,1536]{1,0:T(8,128)(2,1)S(1)} %bitcast.4, bf16[1536,1024]{1,0:T(8,128)(2,1)S(1)} %copy-done, bf16[128,1024]{1,0:T(8,128)(2,1)S(1)} %bitcast.5, s32[1,128]{1,0:T(1,128)S(1)} %copy-done.3, f32[1]{0:T(128)S(6)} %copy.12.log_scale, ...), custom_call_target="tpu_custom_call" | custom-call | tf_op jit(solution)/shard_map/pallas_call | solution.py:310
  70.2 0.5 copy.14
  70.8 0.7 copy.15
  71.4 0.8 %copy.16 = f32[1,128,1024]{2,1,0:T(8,128)} copy(f32[1,128,1024]{2,1,0:T(8,128)S(1)} %bitcast.3) | data formatting | bytes 1048576
Async XLA Ops:
  1.9 1.9 %copy-start = (bf16[1536,1024]{1,0:T(8,128)(2,1)S(1)}, bf16[1536,1024]{1,0:T(8,128)(2,1)}, u32[]{:S(2)}) copy-start(bf16[1536,1024]{1,0:T(8,128)(2,1)} %w_hbm.1) | copy-start | bytes 9437188
  3.8 1.0 %copy-start.1 = (bf16[1,128,1536]{2,1,0:T(8,128)(2,1)S(1)}, bf16[1,128,1536]{2,1,0:T(8,128)(2,1)}, u32[]{:S(2)}) copy-start(bf16[1,128,1536]{2,1,0:T(8,128)(2,1)} %param.6) | copy-start | bytes 1179652
  4.8 0.9 %copy-start.2 = (bf16[1,128,1024]{2,1,0:T(8,128)(2,1)S(1)}, bf16[1,128,1024]{2,1,0:T(8,128)(2,1)}, u32[]{:S(2)}) copy-start(bf16[1,128,1024]{2,1,0:T(8,128)(2,1)} %param.8) | copy-start | bytes 786436
  5.8 0.7 copy-start.3

commit v2 on v1

--- a/solution.py
+++ b/solution.py
@@ -10,16 +10,17 @@
 LINE = 4
 QUAD = 4
 LAYER = 8
+PARTS = 4
 
 
 def fused_kernel(
-    pooled, w_hbm, text_in, pos_in, log_scale, bias,
+    pooled_hbm, w_hbm, text_hbm, pos_hbm, log_scale, bias,
     loss_out, weight_out, text_out,
-    w, text_all, image_all, pos_all, pt_send, pt_all,
+    pooled, w, text_in, pos_in, text_all, image_all, pos_all, pt_send, pt_all,
     text_unit, image_unit, td_own, td_send, td_recv, id_acc, id_send, id_recv, id_far, id_far_recv,
-    loss_part, loss_recv, ib_all, weight_own, wp_send, wp_recv,
-    w_sem, tg_s, tg_f, tg_r, ig_s, ig_r, pg_s, pg_r, pt_s, pt_r, td_s, td_r,
-    id_s, id_r, ls_s, ls_r, ib_s, ib_f, ib_r, wp_s, wp_r,
+    coeff_parts, loss_part, loss_recv, ib_all, weight_own, wp_send, wp_recv,
+    in_sem, tg_s, tg_f, tg_r, ig_s, ig_r, pg_s, pg_r, pt_s, pt_r, td_s, td_r,
+    id_s, id_r, ls_s, ls_r, ib_s, ib_f, ib_d, ib_r, wp_s, wp_r,
 ):
     blk, x = lax.axis_index("blk"), lax.axis_index("rep")
     z, y, c = blk // 4, (blk // 2) % 2, blk % 2
@@ -50,8 +51,10 @@
 
     order = [flip(mid), flip(1 - mid), flip(2), flip(3)]
 
-    w_copy = pltpu.make_async_copy(w_hbm, w, w_sem)
-    w_copy.start()
+    ins = [(text_hbm, text_in), (pos_hbm, pos_in), (pooled_hbm, pooled), (w_hbm, w)]
+    ins = [pltpu.make_async_copy(src, dst, in_sem.at[k]) for k, (src, dst) in enumerate(ins)]
+    for copy in ins:
+        copy.start()
     barrier = pltpu.get_barrier_semaphore()
     for k in range(1, LAYER):
         pl.semaphore_signal(barrier, inc=1, device_id=layer_dev((me + k) % LAYER), device_id_type=pl.DeviceIdType.MESH)
@@ -60,11 +63,13 @@
             barrier, inc=1, device_id=dev((z + k) % LINE, y, c, x), device_id_type=pl.DeviceIdType.MESH
         )
 
+    ins[0].wait()
     raw = text_in[...].astype(F32)
     text_inv = lax.rsqrt(jnp.sum(raw * raw, axis=-1, keepdims=True) + 1e-06)
     unit = raw * text_inv
     text_unit[...] = unit
     text_all[z] = unit.astype(BF16)
+    ins[1].wait()
     pos_all[q] = pos_in[...]
     pl.semaphore_wait(barrier, LAYER - 1 + LINE - 1)
 
@@ -84,7 +89,8 @@
     for copy in pos_copies:
         copy.start()
 
-    w_copy.wait()
+    ins[2].wait()
+    ins[3].wait()
     projected = jnp.dot(pooled[...], w[...], preferred_element_type=F32)
     image_inv = lax.rsqrt(jnp.sum(projected * projected, axis=-1, keepdims=True) + 1e-06)
     unit = projected * image_inv
@@ -107,9 +113,6 @@
         j = (me + k) % LAYER
         return remote(pt_send.at[j], pt_all.at[me], pt_s.at[j], pt_r.at[me], layer_dev(j))
 
-    for k in range(1, LAYER):
-        pt_copy(k).start()
-
     def forward(i):
         s = order[i]
         slot = text_all.at[s]
@@ -144,6 +147,9 @@
     image_pass.start()
     image_slot(0, y, oc).wait_recv()
     image_slot(0, oy, oc).wait_recv()
+
+    for k in range(1, LAYER):
+        pt_copy(k).start()
 
     images = image_all[...].reshape(QUAD * rows, emb)
     pos = jnp.concatenate([pos_all[k] for k in range(QUAD)], axis=1)
@@ -175,12 +181,21 @@
             jnp.maximum(value, 0.0) + jnp.log1p(jnp.exp(-jnp.abs(value))), axis=0, keepdims=True
         )
         coeffs = (-sign * jax.nn.sigmoid(value) * scale).astype(BF16)
+        if i == LINE - 1:
+            break
         text_part = jnp.dot(coeffs, images, preferred_element_type=F32)
         if i == 0:
             td_own[...] = text_part
         else:
             td_send[s] = text_part.astype(BF16)
-            text_dir_copy(i).start()
+        if i == 1:
+
+            @pl.when(mid == 0)
+            def _():
+                text_dir_copy(1).start()
+
+        if i == 2:
+            text_dir_copy(2).start()
         image_part = lax.dot_general(
             coeffs, text, (((0,), (0,)), ((), ())), preferred_element_type=F32
         ).reshape(QUAD, rows, emb)
@@ -189,52 +204,63 @@
         else:
             id_acc[...] += image_part
 
-    id_send[1] = id_acc[oy * 2 + oc].astype(BF16)
+    for k in range(QUAD):
+        coeff_parts[k] = coeffs[:, k * rows : (k + 1) * rows]
+        loss_part[k] = losses[:, k * rows : (k + 1) * rows]
+
+    def image_sum(yy, cc):
+        return id_acc[yy * 2 + cc] + lax.dot_general(
+            coeff_parts[yy * 2 + cc], text, (((0,), (0,)), ((), ())), preferred_element_type=F32
+        )
+
     pair = dev(z, y, oc, x)
     id_copies = [remote(id_send.at[k], id_recv.at[k], id_s.at[k], id_r.at[k], pair) for k in range(2)]
+    id_send[1] = image_sum(oy, oc).astype(BF16)
     id_copies[1].start()
-    id_send[0] = id_acc[y * 2 + oc].astype(BF16)
+    id_send[0] = image_sum(y, oc).astype(BF16)
     id_copies[0].start()
-    for k in range(QUAD):
-        loss_part[k] = losses[:, k * rows : (k + 1) * rows]
+    id_acc[oy * 2 + c] = image_sum(oy, c)
+    id_copies[1].wait_recv()
+    id_far[...] = (id_acc[oy * 2 + c] + id_recv[1].astype(F32)).astype(BF16)
+    far_copy = remote(id_far, id_far_recv, id_s.at[2], id_r.at[2], dev(z, oy, c, x))
+    far_copy.start()
+    near = image_sum(y, c)
+    td_send[s] = jnp.dot(coeffs, images, preferred_element_type=F32).astype(BF16)
+
+    @pl.when(mid == 1)
+    def _():
+        text_dir_copy(1).start()
+
+    text_dir_copy(3).start()
     loss_copies = [
         remote(loss_part.at[yy * 2 + cc], loss_recv.at[q], ls_s.at[k], ls_r.at[q], dev(z, yy, cc, x))
         for k, (yy, cc) in enumerate(peers)
     ]
     for copy in loss_copies:
         copy.start()
-    id_copies[1].wait_recv()
-    id_far[...] = (id_acc[oy * 2 + c] + id_recv[1].astype(F32)).astype(BF16)
-    far_copy = remote(id_far, id_far_recv, id_s.at[2], id_r.at[2], dev(z, oy, c, x))
-    far_copy.start()
     id_copies[0].wait_recv()
-    near = id_acc[q] + id_recv[0].astype(F32)
+    near += id_recv[0].astype(F32)
     far_copy.wait_recv()
     image_dir = near + id_far_recv[...].astype(F32)
     unit = image_unit[...]
-    ib_all[me] = (
+    image_back = (
         (image_dir - unit * jnp.sum(unit * image_dir, axis=-1, keepdims=True)) * image_inv
     ).astype(BF16)
-
-    others = [(oy, c, ox), (oy, c, x), (y, c, ox), (y, oc, x)]
+    part = emb // PARTS
+    for k in range(PARTS):
+        ib_all[k, me] = image_back[:, k * part : (k + 1) * part]
+
+    def ib_copy(k, slot, send, *to):
+        j = layer_of(*slot)
+        return remote(ib_all.at[k, j], ib_all.at[k, j], send, ib_r.at[k, j], dev(z, *to))
+
+    own, pair, by_y, by_x, diagonal = (y, c, x), (y, oc, x), (oy, c, x), (y, c, ox), (oy, c, ox)
     ib_copies = [
-        remote(ib_all.at[me], ib_all.at[me], ib_s.at[k], ib_r.at[me], dev(z, *other))
-        for k, other in enumerate(others)
+        ib_copy(k, own, ib_s.at[k, n], *to) for k in range(PARTS) for n, to in enumerate((by_x, by_y, pair))
     ]
     for copy in ib_copies:
         copy.start()
 
-    def ib_slot(k, *other):
-        slot = ib_all.at[layer_of(*other)]
-        return remote(slot, slot, ib_f.at[k], ib_r.at[layer_of(*other)], pair)
-
-    ib_passes = [ib_slot(k, *other) for k, other in enumerate([(oy, c, x), (y, c, ox), (oy, c, ox)])]
-    for copy in ib_passes:
-        copy.wait_recv()
-        copy.start()
-    for other in [(y, oc, x), (oy, oc, x), (y, oc, ox), (oy, oc, ox)]:
-        ib_slot(0, *other).wait_recv()
-
     def pt_recv(k):
         j = (me + k) % LAYER
         return remote(pt_all.at[j], pt_all.at[j], pt_s.at[j], pt_r.at[j], layer_dev(j))
@@ -244,26 +270,46 @@
 
     share = pt_all.shape[2]
     turned_all = jnp.concatenate([pt_all[j].reshape(LINE * share, rows) for j in range(LAYER)], axis=1)
-    weight_part = jnp.dot(turned_all, ib_all[...].reshape(LAYER * rows, emb), preferred_element_type=F32)
-    for t in range(LINE):
-        weight_own[t] = weight_part[t * share : (t + 1) * share]
-        wp_send[t] = weight_part[t * share : (t + 1) * share].astype(BF16)
-
-    def weight_copy(k):
-        t = (z + k) % LINE
-        return remote(wp_send.at[t], wp_recv.at[z], wp_s.at[t], wp_r.at[z], dev(t, y, c, x))
-
-    def from_line(recv, sem, k):
-        t = (z + k) % LINE
-        return remote(recv.at[t], recv.at[t], wp_s.at[t], sem.at[t], dev(t, y, c, x))
-
-    for k in range(1, LINE):
-        weight_copy(k).start()
+
+    def weight_copy(k, n):
+        t = (z + n) % LINE
+        return remote(wp_send.at[k, t], wp_recv.at[k, z], wp_s.at[k, t], wp_r.at[k, z], dev(t, y, c, x))
+
+    for step in range(PARTS + 2):
+        k = step
+        if k < PARTS:
+            for n, slot in enumerate((by_x, by_y)):
+                ib_copy(k, slot, ib_f.at[k, n], *pair).wait_recv()
+                if k % 2 == n:
+                    on = ib_copy(k, slot, ib_d.at[k], *(by_y if n == 0 else by_x))
+                    on.start()
+                    ib_copies.append(on)
+                on = ib_copy(k, slot, ib_f.at[k, n], *pair)
+                on.start()
+                ib_copies.append(on)
+        k = step - 1
+        if 0 <= k < PARTS:
+            on = ib_copy(k, diagonal, ib_f.at[k, 2], *pair)
+            on.wait_recv()
+            on.start()
+            ib_copies.append(on)
+        k = step - 2
+        if k < 0:
+            continue
+        for slot in ((y, oc, x), (oy, oc, x), (y, oc, ox), (oy, oc, ox)):
+            ib_copy(k, slot, ib_f.at[k, 0], *pair).wait_recv()
+        product = jnp.dot(turned_all, ib_all[k].reshape(LAYER * rows, part), preferred_element_type=F32)
+        for t in range(LINE):
+            weight_own[k, t] = product[t * share : (t + 1) * share]
+            wp_send[k, t] = product[t * share : (t + 1) * share].astype(BF16)
+        for n in range(1, LINE):
+            weight_copy(k, n).start()
 
     total = td_own[...]
     for k in range(1, LINE):
-        from_line(td_recv, td_r, k).wait_recv()
-        total += td_recv[(z + k) % LINE].astype(F32)
+        t = (z + k) % LINE
+        remote(td_recv.at[t], td_recv.at[t], td_s.at[t], td_r.at[t], dev(t, y, c, x)).wait_recv()
+        total += td_recv[t].astype(F32)
     unit = text_unit[...]
     text_out[...] = (total - unit * jnp.sum(unit * total, axis=-1, keepdims=True)) * text_inv
 
@@ -274,11 +320,14 @@
         total += loss_recv[qq]
     loss_out[...] = total / (LINE * QUAD * rows)
 
-    total = weight_own[z]
-    for k in range(1, LINE):
-        from_line(wp_recv, wp_r, k).wait_recv()
-        total += wp_recv[(z + k) % LINE].astype(F32)
-    weight_out[...] = total / 64.0
+    for k in range(PARTS):
+        total = weight_own[k, z]
+        for n in range(1, LINE):
+            t = (z + n) % LINE
+            slot = wp_recv.at[k, t]
+            remote(slot, slot, wp_s.at[k, t], wp_r.at[k, t], dev(t, y, c, x)).wait_recv()
+            total += wp_recv[k, t].astype(F32)
+        weight_out[:, k * part : (k + 1) * part] = total / 64.0
 
     own_a.wait_send()
 
@@ -290,13 +339,14 @@
 
     for copy in pos_copies + image_copies + [image_pass] + id_copies + [far_copy] + loss_copies:
         copy.wait_send()
-    for copy in ib_copies + ib_passes:
+    for copy in ib_copies:
         copy.wait_send()
     for k in range(1, LAYER):
         pt_copy(k).wait_send()
     for k in range(1, LINE):
         text_dir_copy(k).wait_send()
-        weight_copy(k).wait_send()
+        for part in range(PARTS):
+            weight_copy(part, k).wait_send()
 
 
 def fused(pooled, w_img, text_emb, pos_index, log_scale, bias):
@@ -305,6 +355,7 @@
     share = width // (LINE * LAYER)
     vmem, dma = pltpu.VMEM, pltpu.SemaphoreType.DMA
     in_vmem = pl.BlockSpec(memory_space=pltpu.VMEM)
+    in_hbm = pl.BlockSpec(memory_space=pltpu.HBM)
     in_smem = pl.BlockSpec(memory_space=pltpu.SMEM)
     block = (rows, emb)
     loss, weight, text = pl.pallas_call(
@@ -314,10 +365,13 @@
             jax.ShapeDtypeStruct((share, emb), F32),
             jax.ShapeDtypeStruct(block, F32),
         ),
-        in_specs=[in_vmem, pl.BlockSpec(memory_space=pl.ANY), in_vmem, in_vmem, in_smem, in_smem],
+        in_specs=[in_hbm, in_hbm, in_hbm, in_hbm, in_smem, in_smem],
         out_specs=(in_vmem, in_vmem, in_vmem),
         scratch_shapes=[
+            vmem((rows, width), BF16),
             vmem((width, emb), BF16),
+            vmem(block, BF16),
+            vmem((1, rows), jnp.int32),
             vmem((LINE,) + block, BF16),
             vmem((QUAD,) + block, BF16),
             vmem((QUAD, 1, rows), jnp.int32),
@@ -333,13 +387,14 @@
             vmem((2,) + block, BF16),
             vmem(block, BF16),
             vmem(block, BF16),
+            vmem((QUAD, rows, rows), BF16),
             vmem((QUAD, 1, rows), F32),
             vmem((QUAD, 1, rows), F32),
-            vmem((LAYER,) + block, BF16),
-            vmem((LINE, share, emb), F32),
-            vmem((LINE, share, emb), BF16),
-            vmem((LINE, share, emb), BF16),
-            dma,
+            vmem((PARTS, LAYER, rows, emb // PARTS), BF16),
+            vmem((PARTS, LINE, share, emb // PARTS), F32),
+            vmem((PARTS, LINE, share, emb // PARTS), BF16),
+            vmem((PARTS, LINE, share, emb // PARTS), BF16),
+            dma((4,)),
             dma((2,)), dma((LINE,)), dma((LINE,)),
             dma((3,)), dma((QUAD,)),
             dma((3,)), dma((QUAD,)),
@@ -347,11 +402,11 @@
             dma((LINE,)), dma((LINE,)),
             dma((3,)), dma((3,)),
             dma((3,)), dma((QUAD,)),
-            dma((4,)), dma((3,)), dma((LAYER,)),
-            dma((LINE,)), dma((LINE,)),
+            dma((PARTS, 3)), dma((PARTS, 3)), dma((PARTS,)), dma((PARTS, LAYER)),
+            dma((PARTS, LINE)), dma((PARTS, LINE)),
         ],
         compiler_params=pltpu.CompilerParams(
-            collective_id=0, has_side_effects=True, vmem_limit_bytes=48 * 2**20
+            collective_id=0, has_side_effects=True, vmem_limit_bytes=63 * 2**20
         ),
     )(pooled[0], w_img, text_emb[0], pos_index, log_scale, bias)
     return loss, weight, text[None]

time: 72.5 us -> 66.2 us (0.913)
  Pallas kernels: 63.8 us -> 59.5 us
  local copies, waits for them, and re-layouts: 6.46 us -> 4.62 us
    pallas_call x1, Pallas kernels: 63.8 us -> 59.5 us  [fused(): pl.pallas_call(fused_kernel, out_shape=(jax.ShapeDtypeStruct((1, rows), F...]
    unnamed x11 -> x3, local copies, waits for them, and re-layouts: 6.46 us -> 4.62 us
where the time goes in v2:
time: 66.2 us; the launch traced here: 66 us
  Pallas kernels  59.5 us (90%)
  local copies, waits for them, and re-layouts  4.62 us (7%)
  between operations  1.93 us (3%)
    pallas_call x1, Pallas kernels, fused(): pl.pallas_call(fused_kernel, out_shape=(jax.ShapeDtypeStruct((1, rows), F...  59.5 us
    unnamed x3, local copies, waits for them, and re-layouts  4.62 us

profile of v2, /device:TPU:0, one launch (start us, length us, event | category | flops | bytes accessed | tf_op | source)
XLA Modules:
  0.0 66.0 jit_solution(6465921965155569858)
XLA Ops:
  1.9 59.5 %shard_map.85 = (f32[1,128]{1,0:T(1,128)}, f32[48,1024]{1,0:T(8,128)}, f32[128,1024]{1,0:T(8,128)}) custom-call(bf16[128,1536]{1,0:T(8,128)(2,1)} %bitcast.4, bf16[1536,1024]{1,0:T(8,128)(2,1)} %w_hbm.1, bf16[128,1024]{1,0:T(8,128)(2,1)} %bitcast.5, s32[1,128]{1,0:T(1,128)} %pos_hbm.1, f32[1]{0:T(128)S(6)} %copy.12.log_scale, f32[1]{0:T(128)S(6)} %copy.13.bias), custom_call_target="tpu_custom_call" | custom-call | tf_op jit(solution)/shard_map/pallas_call | solution.py:361
  61.4 1.1 %copy.14 = f32[1,128]{1,0:T(1,128)} copy(f32[1,128]{1,0:T(1,128)} %get-tuple-element.12) | data formatting | bytes 1024
  62.5 1.6 %copy.15 = f32[48,1024]{1,0:T(8,128)} copy(f32[48,1024]{1,0:T(8,128)} %get-tuple-element.13) | data formatting | bytes 393216
  64.1 1.9 %copy.16 = f32[1,128,1024]{2,1,0:T(8,128)} copy(f32[1,128,1024]{2,1,0:T(8,128)} %bitcast.3) | data formatting | bytes 1048576

commit v3 on v2

--- a/solution.py
+++ b/solution.py
@@ -10,6 +10,7 @@
 LINE = 4
 QUAD = 4
 LAYER = 8
+PIECES = 4
 PARTS = 4
 
 
@@ -17,9 +18,9 @@
     pooled_hbm, w_hbm, text_hbm, pos_hbm, log_scale, bias,
     loss_out, weight_out, text_out,
     pooled, w, text_in, pos_in, text_all, image_all, pos_all, pt_send, pt_all,
-    text_unit, image_unit, td_own, td_send, td_recv, id_acc, id_send, id_recv, id_far, id_far_recv,
+    text_unit, image_unit, td_acc, td_send, td_recv, id_acc, id_send, id_recv, id_far, id_far_recv,
     coeff_parts, loss_part, loss_recv, ib_all, weight_own, wp_send, wp_recv,
-    in_sem, tg_s, tg_f, tg_r, ig_s, ig_r, pg_s, pg_r, pt_s, pt_r, td_s, td_r,
+    in_sem, tg_s, tg_f, tg_y, tg_r, ig_s, ig_r, pg_s, pg_r, pt_s, pt_r, td_s, td_r,
     id_s, id_r, ls_s, ls_r, ib_s, ib_f, ib_d, ib_r, wp_s, wp_r,
 ):
     blk, x = lax.axis_index("blk"), lax.axis_index("rep")
@@ -42,14 +43,10 @@
             device_id=device, device_id_type=pl.DeviceIdType.MESH,
         )
 
-    q, me = y * 2 + c, layer_of(y, c, x)
-    far = z // 2
-    mid = z * (1 - far) + (LINE - 1 - z) * far
-
-    def flip(base):
-        return base + far * (LINE - 1 - 2 * base)
-
-    order = [flip(mid), flip(1 - mid), flip(2), flip(3)]
+    half, odd = z // 2, z % 2
+    other_half, other_odd = 1 - half, 1 - odd
+    z_far, z_near = other_half * 2 + odd, half * 2 + other_odd
+    me = layer_of(y, c, x)
 
     ins = [(text_hbm, text_in), (pos_hbm, pos_in), (pooled_hbm, pooled), (w_hbm, w)]
     ins = [pltpu.make_async_copy(src, dst, in_sem.at[k]) for k, (src, dst) in enumerate(ins)]
@@ -62,29 +59,42 @@
         pl.semaphore_signal(
             barrier, inc=1, device_id=dev((z + k) % LINE, y, c, x), device_id_type=pl.DeviceIdType.MESH
         )
+    pl.semaphore_signal(barrier, inc=1, device_id=dev(z_near, y, oc, x), device_id_type=pl.DeviceIdType.MESH)
 
     ins[0].wait()
     raw = text_in[...].astype(F32)
     text_inv = lax.rsqrt(jnp.sum(raw * raw, axis=-1, keepdims=True) + 1e-06)
     unit = raw * text_inv
     text_unit[...] = unit
-    text_all[z] = unit.astype(BF16)
+    text_all[half, y] = unit.astype(BF16)
     ins[1].wait()
-    pos_all[q] = pos_in[...]
-    pl.semaphore_wait(barrier, LAYER - 1 + LINE - 1)
-
-    own_a = remote(text_all.at[z], text_all.at[z], tg_s.at[0], tg_r.at[z], dev(flip(1 + mid), y, c, x))
-    own_b = remote(text_all.at[z], text_all.at[z], tg_s.at[1], tg_r.at[z], dev(flip(0), y, c, x))
-    own_a.start()
-
-    @pl.when(mid == 1)
-    def _():
-        own_b.start()
-
-    peers = [(y, oc), (oy, c), (oy, oc)]
+    pos_all[odd, c] = pos_in[...]
+    pl.semaphore_wait(barrier, LAYER - 1 + LINE)
+
+    piece = rows // PIECES
+
+    def text_piece(hh, yy, k, send, *to):
+        slot = text_all.at[hh, yy, pl.ds(k * piece, piece)]
+        return remote(slot, slot, send, tg_r.at[hh, yy, k], dev(*to))
+
+    far_texts = [text_piece(half, y, k, tg_s.at[k], z_far, y, c, x) for k in range(PIECES)]
+    for copy in far_texts:
+        copy.start()
+
+    def text_whole(yy):
+        slot = text_all.at[half, yy]
+        return remote(slot, slot, tg_y, tg_r.at[half, yy, 0], dev(z, oy, c, x))
+
+    text_whole(y).start()
+
+    peers = [(odd, oc), (other_odd, c), (other_odd, oc)]
+
+    def peer_dev(oo, cc):
+        return dev(half * 2 + oo, y, cc, x)
+
     pos_copies = [
-        remote(pos_all.at[q], pos_all.at[q], pg_s.at[k], pg_r.at[q], dev(z, yy, cc, x))
-        for k, (yy, cc) in enumerate(peers)
+        remote(pos_all.at[odd, c], pos_all.at[odd, c], pg_s.at[k], pg_r.at[odd, c], peer_dev(*peer))
+        for k, peer in enumerate(peers)
     ]
     for copy in pos_copies:
         copy.start()
@@ -95,11 +105,13 @@
     image_inv = lax.rsqrt(jnp.sum(projected * projected, axis=-1, keepdims=True) + 1e-06)
     unit = projected * image_inv
     image_unit[...] = unit
-    image_all[q] = unit.astype(BF16)
-    image_copies = [
-        remote(image_all.at[q], image_all.at[q], ig_s.at[k], ig_r.at[q], dev(z, yy, cc, x))
-        for k, (yy, cc) in enumerate(peers[:2])
-    ]
+    image_all[odd, c] = unit.astype(BF16)
+
+    def image_copy(k, oo, cc, to):
+        slot = image_all.at[oo, cc]
+        return remote(slot, slot, ig_s.at[k], ig_r.at[oo, cc], peer_dev(*to))
+
+    image_copies = [image_copy(k, odd, c, to) for k, to in enumerate(peers[:2])]
     image_copies[1].start()
     image_copies[0].start()
 
@@ -113,128 +125,108 @@
         j = (me + k) % LAYER
         return remote(pt_send.at[j], pt_all.at[me], pt_s.at[j], pt_r.at[me], layer_dev(j))
 
-    def forward(i):
-        s = order[i]
-        slot = text_all.at[s]
-        return remote(slot, slot, tg_f.at[i], tg_r.at[s], dev(flip(2 if i == 1 else 0), y, c, x))
-
-    def arrive(i):
-        copy = forward(i)
-        copy.wait_recv()
-
-        @pl.when(mid == 1)
-        def _():
-            copy.start()
-
-    arrive(1)
-
-    @pl.when(mid == 1)
-    def _():
-        copy = forward(2)
-        copy.wait_recv()
-        copy.start()
-
-    for k, (yy, cc) in enumerate(peers):
-        qq = yy * 2 + cc
-        remote(pos_all.at[qq], pos_all.at[qq], pg_s.at[k], pg_r.at[qq], dev(z, yy, cc, x)).wait_recv()
-
-    def image_slot(k, yy, cc):
-        slot = image_all.at[yy * 2 + cc]
-        return remote(slot, slot, ig_s.at[k], ig_r.at[yy * 2 + cc], dev(z, y, oc, x))
-
-    image_pass = image_slot(2, oy, c)
-    image_pass.wait_recv()
-    image_pass.start()
-    image_slot(0, y, oc).wait_recv()
-    image_slot(0, oy, oc).wait_recv()
-
-    for k in range(1, LAYER):
-        pt_copy(k).start()
-
-    images = image_all[...].reshape(QUAD * rows, emb)
-    pos = jnp.concatenate([pos_all[k] for k in range(QUAD)], axis=1)
-    scale = jnp.exp(jnp.full((1, QUAD * rows), log_scale[0], F32))
+    scale = jnp.exp(jnp.full((1, 2 * rows), log_scale[0], F32))
     shift = bias[0]
-    losses = jnp.zeros((1, QUAD * rows), F32)
-
-    def text_dir_copy(i):
-        s = order[i]
-        return remote(td_send.at[s], td_recv.at[z], td_s.at[s], td_r.at[z], dev(s, y, c, x))
-
-    for i in range(LINE):
-        if i == 2:
-
-            @pl.when(mid == 0)
-            def _():
-                forward(2).wait_recv()
-
-        if i == 3:
-            arrive(3)
-        s = order[i]
-        text = text_all[s]
+
+    def pairs(owners, oo):
+        text = jnp.concatenate([text_all[hh, yy] for hh, yy in owners], axis=0)
+        images = image_all[oo].reshape(2 * rows, emb)
+        pos = jnp.concatenate([pos_all[oo, 0], pos_all[oo, 1]], axis=1)
         dots = lax.dot_general(text, images, (((1,), (1,)), ((), ())), preferred_element_type=F32)
         logits = scale * dots + shift
-        owner = (s * QUAD + q) * rows + lax.broadcasted_iota(jnp.int32, (rows, QUAD * rows), 0)
-        sign = jnp.where(owner == pos, 1.0, -1.0).astype(F32)
+        index = lax.broadcasted_iota(jnp.int32, (rows, 2 * rows), 0)
+        index = jnp.concatenate([((hh * 2 + odd) * 4 + yy * 2 + c) * rows + index for hh, yy in owners], axis=0)
+        sign = jnp.where(index == pos, 1.0, -1.0).astype(F32)
         value = -sign * logits
-        losses += jnp.sum(
+        losses = jnp.sum(
             jnp.maximum(value, 0.0) + jnp.log1p(jnp.exp(-jnp.abs(value))), axis=0, keepdims=True
         )
         coeffs = (-sign * jax.nn.sigmoid(value) * scale).astype(BF16)
-        if i == LINE - 1:
-            break
-        text_part = jnp.dot(coeffs, images, preferred_element_type=F32)
-        if i == 0:
-            td_own[...] = text_part
-        else:
-            td_send[s] = text_part.astype(BF16)
-        if i == 1:
-
-            @pl.when(mid == 0)
-            def _():
-                text_dir_copy(1).start()
-
-        if i == 2:
-            text_dir_copy(2).start()
-        image_part = lax.dot_general(
-            coeffs, text, (((0,), (0,)), ((), ())), preferred_element_type=F32
-        ).reshape(QUAD, rows, emb)
-        if i == 0:
-            id_acc[...] = image_part
-        else:
-            id_acc[...] += image_part
-
-    for k in range(QUAD):
-        coeff_parts[k] = coeffs[:, k * rows : (k + 1) * rows]
-        loss_part[k] = losses[:, k * rows : (k + 1) * rows]
-
-    def image_sum(yy, cc):
-        return id_acc[yy * 2 + cc] + lax.dot_general(
-            coeff_parts[yy * 2 + cc], text, (((0,), (0,)), ((), ())), preferred_element_type=F32
-        )
+        return text, images, coeffs, losses
+
+    def text_terms(coeffs, images):
+        return jnp.dot(coeffs, images, preferred_element_type=F32)
+
+    def image_terms(coeffs, text):
+        return lax.dot_general(coeffs, text, (((0,), (0,)), ((), ())), preferred_element_type=F32)
+
+    here, by_y, ahead, across = (half, y), (half, oy), (other_half, y), (other_half, oy)
+
+    for k, peer in enumerate(peers):
+        remote(pos_all.at[peer], pos_all.at[peer], pg_s.at[k], pg_r.at[peer], peer_dev(*peer)).wait_recv()
+    text_whole(oy).wait_recv()
+    image_copy(0, odd, oc, peers[0]).wait_recv()
+    text, images, coeffs, loss_here = pairs([here, by_y], odd)
+    terms = text_terms(coeffs, images)
+    td_acc[here] = terms[:rows]
+    td_acc[by_y] = terms[rows:]
+    id_acc[odd] = image_terms(coeffs, text).reshape(2, rows, emb)
+
+    text_passes = []
+    for k in range(PIECES):
+        copy = text_piece(*ahead, k, tg_f.at[k], z, oy, c, x)
+        copy.wait_recv()
+        copy.start()
+        text_passes.append(copy)
+    text, images, coeffs, losses = pairs([ahead], odd)
+    loss_here += losses
+    td_acc[ahead] = text_terms(coeffs, images)
+    id_acc[odd] += image_terms(coeffs, text).reshape(2, rows, emb)
+
+    image_pass = image_copy(2, other_odd, c, peers[0])
+    image_pass.wait_recv()
+    image_pass.start()
+    for k in range(1, LAYER):
+        pt_copy(k).start()
+    image_copy(0, other_odd, oc, peers[0]).wait_recv()
+    text, images, coeffs, loss_near = pairs([here, by_y, ahead], other_odd)
+    terms = text_terms(coeffs, images)
+    td_send[0] = (td_acc[by_y] + terms[rows : 2 * rows]).astype(BF16)
+
+    def td_copy(k, *to):
+        return remote(td_send.at[k], td_recv.at[k], td_s.at[k], td_r.at[k], dev(*to))
+
+    td_copies = [td_copy(0, z, oy, c, x), td_copy(1, z, oy, c, x), td_copy(2, z_far, y, c, x)]
+    td_copies[0].start()
+    td_acc[here] += terms[:rows]
+    td_acc[ahead] += terms[2 * rows :]
+    id_acc[other_odd] = image_terms(coeffs, text).reshape(2, rows, emb)
+
+    for k in range(PIECES):
+        text_piece(*across, k, tg_f.at[k], z, oy, c, x).wait_recv()
+
+    def image_sum(oo, cc):
+        return id_acc[oo, cc] + image_terms(coeff_parts[oo, cc], text)
 
     pair = dev(z, y, oc, x)
     id_copies = [remote(id_send.at[k], id_recv.at[k], id_s.at[k], id_r.at[k], pair) for k in range(2)]
-    id_send[1] = image_sum(oy, oc).astype(BF16)
+    text, images, coeffs, losses = pairs([across], other_odd)
+    loss_near += losses
+    for k in range(2):
+        coeff_parts[other_odd, k] = coeffs[:, k * rows : (k + 1) * rows]
+    id_send[1] = image_sum(other_odd, oc).astype(BF16)
     id_copies[1].start()
-    id_send[0] = image_sum(y, oc).astype(BF16)
+    id_acc[other_odd, c] = image_sum(other_odd, c)
+    near_images, near_coeffs = images, coeffs
+    text, images, coeffs, losses = pairs([across], odd)
+    loss_here += losses
+    for k in range(2):
+        coeff_parts[odd, k] = coeffs[:, k * rows : (k + 1) * rows]
+    id_send[0] = image_sum(odd, oc).astype(BF16)
     id_copies[0].start()
-    id_acc[oy * 2 + c] = image_sum(oy, c)
+    for k in range(2):
+        loss_part[odd, k] = loss_here[:, k * rows : (k + 1) * rows]
+        loss_part[other_odd, k] = loss_near[:, k * rows : (k + 1) * rows]
     id_copies[1].wait_recv()
-    id_far[...] = (id_acc[oy * 2 + c] + id_recv[1].astype(F32)).astype(BF16)
-    far_copy = remote(id_far, id_far_recv, id_s.at[2], id_r.at[2], dev(z, oy, c, x))
+    id_far[...] = (id_acc[other_odd, c] + id_recv[1].astype(F32)).astype(BF16)
+    far_copy = remote(id_far, id_far_recv, id_s.at[2], id_r.at[2], dev(z_near, y, c, x))
     far_copy.start()
-    near = image_sum(y, c)
-    td_send[s] = jnp.dot(coeffs, images, preferred_element_type=F32).astype(BF16)
-
-    @pl.when(mid == 1)
-    def _():
-        text_dir_copy(1).start()
-
-    text_dir_copy(3).start()
+    td_send[1] = (text_terms(coeffs, images) + text_terms(near_coeffs, near_images)).astype(BF16)
+    td_copies[1].start()
+    near = image_sum(odd, c)
     loss_copies = [
-        remote(loss_part.at[yy * 2 + cc], loss_recv.at[q], ls_s.at[k], ls_r.at[q], dev(z, yy, cc, x))
-        for k, (yy, cc) in enumerate(peers)
+        remote(loss_part.at[peer], loss_recv.at[odd, c], ls_s.at[k], ls_r.at[odd, c], peer_dev(*peer))
+        for k, peer in enumerate(peers)
     ]
     for copy in loss_copies:
         copy.start()
@@ -267,6 +259,10 @@
 
     for k in range(1, LAYER):
         pt_recv(k).wait_recv()
+
+    td_copies[1].wait_recv()
+    td_send[2] = (td_acc[ahead] + td_recv[1].astype(F32)).astype(BF16)
+    td_copies[2].start()
 
     share = pt_all.shape[2]
     turned_all = jnp.concatenate([pt_all[j].reshape(LINE * share, rows) for j in range(LAYER)], axis=1)
@@ -305,19 +301,17 @@
         for n in range(1, LINE):
             weight_copy(k, n).start()
 
-    total = td_own[...]
-    for k in range(1, LINE):
-        t = (z + k) % LINE
-        remote(td_recv.at[t], td_recv.at[t], td_s.at[t], td_r.at[t], dev(t, y, c, x)).wait_recv()
-        total += td_recv[t].astype(F32)
+    td_copies[0].wait_recv()
+    td_copies[2].wait_recv()
+    total = td_acc[here] + td_recv[0].astype(F32) + td_recv[2].astype(F32)
     unit = text_unit[...]
     text_out[...] = (total - unit * jnp.sum(unit * total, axis=-1, keepdims=True)) * text_inv
 
-    total = loss_part[q]
-    for k, (yy, cc) in enumerate(peers):
-        qq = yy * 2 + cc
-        remote(loss_recv.at[qq], loss_recv.at[qq], ls_s.at[k], ls_r.at[qq], dev(z, yy, cc, x)).wait_recv()
-        total += loss_recv[qq]
+    total = loss_part[odd, c]
+    for k, peer in enumerate(peers):
+        slot = loss_recv.at[peer]
+        remote(slot, slot, ls_s.at[k], ls_r.at[peer], peer_dev(*peer)).wait_recv()
+        total += loss_recv[peer]
     loss_out[...] = total / (LINE * QUAD * rows)
 
     for k in range(PARTS):
@@ -329,22 +323,16 @@
             total += wp_recv[k, t].astype(F32)
         weight_out[:, k * part : (k + 1) * part] = total / 64.0
 
-    own_a.wait_send()
-
-    @pl.when(mid == 1)
-    def _():
-        own_b.wait_send()
-        for i in range(1, LINE):
-            forward(i).wait_send()
-
-    for copy in pos_copies + image_copies + [image_pass] + id_copies + [far_copy] + loss_copies:
+    text_whole(y).wait_send()
+    for copy in far_texts + text_passes + pos_copies + image_copies + [image_pass]:
+        copy.wait_send()
+    for copy in id_copies + [far_copy] + td_copies + loss_copies:
         copy.wait_send()
     for copy in ib_copies:
         copy.wait_send()
     for k in range(1, LAYER):
         pt_copy(k).wait_send()
     for k in range(1, LINE):
-        text_dir_copy(k).wait_send()
         for part in range(PARTS):
             weight_copy(part, k).wait_send()
 
@@ -372,41 +360,41 @@
             vmem((width, emb), BF16),
             vmem(block, BF16),
             vmem((1, rows), jnp.int32),
-            vmem((LINE,) + block, BF16),
-            vmem((QUAD,) + block, BF16),
-            vmem((QUAD, 1, rows), jnp.int32),
+            vmem((2, 2) + block, BF16),
+            vmem((2, 2) + block, BF16),
+            vmem((2, 2, 1, rows), jnp.int32),
             vmem((LAYER, LINE, share, rows), BF16),
             vmem((LAYER, LINE, share, rows), BF16),
             vmem(block, F32),
             vmem(block, F32),
-            vmem(block, F32),
-            vmem((LINE,) + block, BF16),
-            vmem((LINE,) + block, BF16),
-            vmem((QUAD,) + block, F32),
+            vmem((2, 2) + block, F32),
+            vmem((3,) + block, BF16),
+            vmem((3,) + block, BF16),
+            vmem((2, 2) + block, F32),
             vmem((2,) + block, BF16),
             vmem((2,) + block, BF16),
             vmem(block, BF16),
             vmem(block, BF16),
-            vmem((QUAD, rows, rows), BF16),
-            vmem((QUAD, 1, rows), F32),
-            vmem((QUAD, 1, rows), F32),
+            vmem((2, 2, rows, rows), BF16),
+            vmem((2, 2, 1, rows), F32),
+            vmem((2, 2, 1, rows), F32),
             vmem((PARTS, LAYER, rows, emb // PARTS), BF16),
             vmem((PARTS, LINE, share, emb // PARTS), F32),
             vmem((PARTS, LINE, share, emb // PARTS), BF16),
             vmem((PARTS, LINE, share, emb // PARTS), BF16),
             dma((4,)),
-            dma((2,)), dma((LINE,)), dma((LINE,)),
-            dma((3,)), dma((QUAD,)),
-            dma((3,)), dma((QUAD,)),
+            dma((PIECES,)), dma((PIECES,)), dma, dma((2, 2, PIECES)),
+            dma((3,)), dma((2, 2)),
+            dma((3,)), dma((2, 2)),
             dma((LAYER,)), dma((LAYER,)),
-            dma((LINE,)), dma((LINE,)),
             dma((3,)), dma((3,)),
-            dma((3,)), dma((QUAD,)),
+            dma((3,)), dma((3,)),
+            dma((3,)), dma((2, 2)),
             dma((PARTS, 3)), dma((PARTS, 3)), dma((PARTS,)), dma((PARTS, LAYER)),
             dma((PARTS, LINE)), dma((PARTS, LINE)),
         ],
         compiler_params=pltpu.CompilerParams(
-            collective_id=0, has_side_effects=True, vmem_limit_bytes=63 * 2**20
+            collective_id=0, has_side_effects=True, vmem_limit_bytes=61 * 2**20
         ),
     )(pooled[0], w_img, text_emb[0], pos_index, log_scale, bias)
     return loss, weight, text[None]

time: 66.2 us -> 67.7 us (1.023)
  Pallas kernels: 59.5 us -> 60.9 us
    pallas_call x1, Pallas kernels: 59.5 us -> 60.9 us  [fused(): pl.pallas_call(fused_kernel, out_shape=(jax.ShapeDtypeStruct((1, rows), F...]
where the time goes in v3:
time: 67.7 us; the launch traced here: 67.5 us
  Pallas kernels  60.9 us (90%)
  local copies, waits for them, and re-layouts  4.62 us (7%)
  between operations  1.93 us (3%)
    pallas_call x1, Pallas kernels, fused(): pl.pallas_call(fused_kernel, out_shape=(jax.ShapeDtypeStruct((1, rows), F...  60.9 us
    unnamed x3, local copies, waits for them, and re-layouts  4.62 us

profile of v3, /device:TPU:0, one launch (start us, length us, event | category | flops | bytes accessed | tf_op | source)
XLA Modules:
  0.0 67.5 jit_solution(3675199821132236409)
XLA Ops:
  1.9 60.9 %shard_map.85 = (f32[1,128]{1,0:T(1,128)}, f32[48,1024]{1,0:T(8,128)}, f32[128,1024]{1,0:T(8,128)}) custom-call(bf16[128,1536]{1,0:T(8,128)(2,1)} %bitcast.4, bf16[1536,1024]{1,0:T(8,128)(2,1)} %w_hbm.1, bf16[128,1024]{1,0:T(8,128)(2,1)} %bitcast.5, s32[1,128]{1,0:T(1,128)} %pos_hbm.1, f32[1]{0:T(128)S(6)} %copy.12.log_scale, f32[1]{0:T(128)S(6)} %copy.13.bias), custom_call_target="tpu_custom_call" | custom-call | tf_op jit(solution)/shard_map/pallas_call | solution.py:349
  62.9 1.1 %copy.14 = f32[1,128]{1,0:T(1,128)} copy(f32[1,128]{1,0:T(1,128)} %get-tuple-element.12) | data formatting | bytes 1024
  64.0 1.6 %copy.15 = f32[48,1024]{1,0:T(8,128)} copy(f32[48,1024]{1,0:T(8,128)} %get-tuple-element.13) | data formatting | bytes 393216
  65.6 1.9 %copy.16 = f32[1,128,1024]{2,1,0:T(8,128)} copy(f32[1,128,1024]{2,1,0:T(8,128)} %bitcast.3) | data formatting | bytes 1048576

commit v4 on v3

--- a/solution.py
+++ b/solution.py
@@ -187,7 +187,6 @@
         return remote(td_send.at[k], td_recv.at[k], td_s.at[k], td_r.at[k], dev(*to))
 
     td_copies = [td_copy(0, z, oy, c, x), td_copy(1, z, oy, c, x), td_copy(2, z_far, y, c, x)]
-    td_copies[0].start()
     td_acc[here] += terms[:rows]
     td_acc[ahead] += terms[2 * rows :]
     id_acc[other_odd] = image_terms(coeffs, text).reshape(2, rows, emb)
@@ -219,8 +218,14 @@
         loss_part[other_odd, k] = loss_near[:, k * rows : (k + 1) * rows]
     id_copies[1].wait_recv()
     id_far[...] = (id_acc[other_odd, c] + id_recv[1].astype(F32)).astype(BF16)
-    far_copy = remote(id_far, id_far_recv, id_s.at[2], id_r.at[2], dev(z_near, y, c, x))
-    far_copy.start()
+    rows_half = rows // 2
+    halves = [pl.ds(0, rows_half), pl.ds(rows_half, rows_half)]
+    far_copies = [
+        remote(id_far.at[h], id_far_recv.at[h], id_s.at[2 + n], id_r.at[2 + n], dev(z_near, y, c, x))
+        for n, h in enumerate(halves)
+    ]
+    for copy in far_copies:
+        copy.start()
     td_send[1] = (text_terms(coeffs, images) + text_terms(near_coeffs, near_images)).astype(BF16)
     td_copies[1].start()
     near = image_sum(odd, c)
@@ -232,26 +237,36 @@
         copy.start()
     id_copies[0].wait_recv()
     near += id_recv[0].astype(F32)
-    far_copy.wait_recv()
-    image_dir = near + id_far_recv[...].astype(F32)
-    unit = image_unit[...]
-    image_back = (
-        (image_dir - unit * jnp.sum(unit * image_dir, axis=-1, keepdims=True)) * image_inv
-    ).astype(BF16)
+
     part = emb // PARTS
-    for k in range(PARTS):
-        ib_all[k, me] = image_back[:, k * part : (k + 1) * part]
-
-    def ib_copy(k, slot, send, *to):
+    own, by_y, by_x, diagonal = (y, c, x), (oy, c, x), (y, c, ox), (oy, c, ox)
+    cuts = [(pl.ds(0, PARTS // 2), 0), (pl.ds(PARTS // 2, PARTS // 2), 0)]
+    cuts += [(pl.ds(k, 1), 1) for k in range(PARTS)]
+
+    def ib_copy(m, slot, send, *to):
+        columns, n = cuts[m]
         j = layer_of(*slot)
-        return remote(ib_all.at[k, j], ib_all.at[k, j], send, ib_r.at[k, j], dev(z, *to))
-
-    own, pair, by_y, by_x, diagonal = (y, c, x), (y, oc, x), (oy, c, x), (y, c, ox), (oy, c, ox)
-    ib_copies = [
-        ib_copy(k, own, ib_s.at[k, n], *to) for k in range(PARTS) for n, to in enumerate((by_x, by_y, pair))
-    ]
-    for copy in ib_copies:
-        copy.start()
+        ref = ib_all.at[columns, j, halves[n]]
+        return remote(ref, ref, send, ib_r.at[m, j], dev(z, *to))
+
+    ib_copies = []
+    for n in range(2):
+        far_copies[n].wait_recv()
+        lines = slice(n * rows_half, (n + 1) * rows_half)
+        image_dir = near[lines] + id_far_recv[halves[n]].astype(F32)
+        unit = image_unit[halves[n]]
+        image_back = (
+            (image_dir - unit * jnp.sum(unit * image_dir, axis=-1, keepdims=True)) * image_inv[lines]
+        ).astype(BF16)
+        for k in range(PARTS):
+            ib_all[k, me, halves[n]] = image_back[:, k * part : (k + 1) * part]
+        for m, cut in enumerate(cuts):
+            if cut[1] != n:
+                continue
+            for to_n, to in enumerate((by_x, by_y, (y, oc, x))):
+                copy = ib_copy(m, own, ib_s.at[m, to_n], *to)
+                copy.start()
+                ib_copies.append(copy)
 
     def pt_recv(k):
         j = (me + k) % LAYER
@@ -271,29 +286,35 @@
         t = (z + n) % LINE
         return remote(wp_send.at[k, t], wp_recv.at[k, z], wp_s.at[k, t], wp_r.at[k, z], dev(t, y, c, x))
 
-    for step in range(PARTS + 2):
-        k = step
-        if k < PARTS:
+    pair = (y, oc, x)
+    for step in range(len(cuts) + 2):
+        m = step
+        if m < len(cuts):
             for n, slot in enumerate((by_x, by_y)):
-                ib_copy(k, slot, ib_f.at[k, n], *pair).wait_recv()
-                if k % 2 == n:
-                    on = ib_copy(k, slot, ib_d.at[k], *(by_y if n == 0 else by_x))
+                ib_copy(m, slot, ib_f.at[m, n], *pair).wait_recv()
+                if m % 2 == n:
+                    on = ib_copy(m, slot, ib_d.at[m], *(by_y if n == 0 else by_x))
                     on.start()
                     ib_copies.append(on)
-                on = ib_copy(k, slot, ib_f.at[k, n], *pair)
+                on = ib_copy(m, slot, ib_f.at[m, n], *pair)
                 on.start()
                 ib_copies.append(on)
-        k = step - 1
-        if 0 <= k < PARTS:
-            on = ib_copy(k, diagonal, ib_f.at[k, 2], *pair)
+        if m == len(cuts) - 1:
+            td_copies[0].start()
+        m = step - 1
+        if 0 <= m < len(cuts):
+            on = ib_copy(m, diagonal, ib_f.at[m, 2], *pair)
             on.wait_recv()
             on.start()
             ib_copies.append(on)
-        k = step - 2
+        m = step - 2
+        if m < 0:
+            continue
+        for slot in ((y, oc, x), (oy, oc, x), (y, oc, ox), (oy, oc, ox)):
+            ib_copy(m, slot, ib_f.at[m, 0], *pair).wait_recv()
+        k = m - 2
         if k < 0:
             continue
-        for slot in ((y, oc, x), (oy, oc, x), (y, oc, ox), (oy, oc, ox)):
-            ib_copy(k, slot, ib_f.at[k, 0], *pair).wait_recv()
         product = jnp.dot(turned_all, ib_all[k].reshape(LAYER * rows, part), preferred_element_type=F32)
         for t in range(LINE):
             weight_own[k, t] = product[t * share : (t + 1) * share]
@@ -326,7 +347,7 @@
     text_whole(y).wait_send()
     for copy in far_texts + text_passes + pos_copies + image_copies + [image_pass]:
         copy.wait_send()
-    for copy in id_copies + [far_copy] + td_copies + loss_copies:
+    for copy in id_copies + far_copies + td_copies + loss_copies:
         copy.wait_send()
     for copy in ib_copies:
         copy.wait_send()
@@ -335,6 +356,27 @@
     for k in range(1, LINE):
         for part in range(PARTS):
             weight_copy(part, k).wait_send()
+
+
+def settle_kernel(loss_in, weight_in, text_in, loss_out, weight_out, text_out, sems):
+    pairs = [(text_in, text_out), (weight_in, weight_out), (loss_in, loss_out)]
+    copies = [pltpu.make_async_copy(src, dst, sems.at[k]) for k, (src, dst) in enumerate(pairs)]
+    for copy in copies:
+        copy.start()
+    for copy in copies:
+        copy.wait()
+
+
+def settle(*results):
+    anywhere = pl.BlockSpec(memory_space=pl.ANY)
+    return pl.pallas_call(
+        settle_kernel,
+        out_shape=tuple(jax.ShapeDtypeStruct(r.shape, r.dtype) for r in results),
+        in_specs=[anywhere] * len(results),
+        out_specs=(anywhere,) * len(results),
+        scratch_shapes=[pltpu.SemaphoreType.DMA((len(results),))],
+        compiler_params=pltpu.CompilerParams(vmem_limit_bytes=61 * 2**20),
+    )(*results)
 
 
 def fused(pooled, w_img, text_emb, pos_index, log_scale, bias):
@@ -388,15 +430,16 @@
             dma((3,)), dma((2, 2)),
             dma((LAYER,)), dma((LAYER,)),
             dma((3,)), dma((3,)),
-            dma((3,)), dma((3,)),
+            dma((4,)), dma((4,)),
             dma((3,)), dma((2, 2)),
-            dma((PARTS, 3)), dma((PARTS, 3)), dma((PARTS,)), dma((PARTS, LAYER)),
+            dma((PARTS + 2, 3)), dma((PARTS + 2, 3)), dma((PARTS + 2,)), dma((PARTS + 2, LAYER)),
             dma((PARTS, LINE)), dma((PARTS, LINE)),
         ],
         compiler_params=pltpu.CompilerParams(
             collective_id=0, has_side_effects=True, vmem_limit_bytes=61 * 2**20
         ),
     )(pooled[0], w_img, text_emb[0], pos_index, log_scale, bias)
+    loss, weight, text = settle(loss, weight, text)
     return loss, weight, text[None]
 
 

time: 67.7 us -> 85.2 us (1.26)
  Pallas kernels: 60.9 us -> 83.1 us
  local copies, waits for them, and re-layouts: 4.62 us -> 0 us
    pallas_call x0 -> x1, Pallas kernels: none -> 23 us  [settle(): pl.pallas_call(settle_kernel, out_shape=tuple((jax.ShapeDtypeStruct(r.sha...]
    unnamed x3 -> x0, local copies, waits for them, and re-layouts: 4.62 us -> none
where the time goes in v4:
time: 85.2 us; the launch traced here: 85 us
  Pallas kernels  83.1 us (98%)
  between operations  1.93 us (2%)
    pallas_call x1, Pallas kernels, fused(): pl.pallas_call(fused_kernel, out_shape=(jax.ShapeDtypeStruct((1, rows), F...  60.1 us
    pallas_call x1, Pallas kernels, settle(): pl.pallas_call(settle_kernel, out_shape=tuple((jax.ShapeDtypeStruct(r.sha...  23 us

profile of v4, /device:TPU:0, one launch (start us, length us, event | category | flops | bytes accessed | tf_op | source)
XLA Modules:
  0.0 85.0 jit_solution(3658119627239057041)
XLA Ops:
  1.9 60.1 %shard_map.85 = (f32[1,128]{1,0:T(1,128)}, f32[48,1024]{1,0:T(8,128)}, f32[128,1024]{1,0:T(8,128)}) custom-call(bf16[128,1536]{1,0:T(8,128)(2,1)} %bitcast.3, bf16[1536,1024]{1,0:T(8,128)(2,1)} %w_hbm.1, bf16[128,1024]{1,0:T(8,128)(2,1)} %bitcast.4, s32[1,128]{1,0:T(1,128)} %pos_hbm.1, f32[1]{0:T(128)S(6)} %copy.9.log_scale, f32[1]{0:T(128)S(6)} %copy.10.bias), custom_call_target="tpu_custom_call" | custom-call | tf_op jit(solution)/shard_map/pallas_call | solution.py:391
  62.1 23.0 %shard_map.86 = (f32[1,128]{1,0:T(1,128)}, f32[48,1024]{1,0:T(8,128)}, f32[128,1024]{1,0:T(8,128)}) custom-call(f32[1,128]{1,0:T(1,128)} %get-tuple-element.9.loss_in, f32[48,1024]{1,0:T(8,128)} %get-tuple-element.10.weight_in, f32[128,1024]{1,0:T(8,128)} %get-tuple-element.11.text_in), custom_call_target="tpu_custom_call" | custom-call | tf_op jit(solution)/shard_map/pallas_call | solution.py:372

commit v5 on v2

--- a/solution.py
+++ b/solution.py
@@ -17,7 +17,7 @@
     pooled_hbm, w_hbm, text_hbm, pos_hbm, log_scale, bias,
     loss_out, weight_out, text_out,
     pooled, w, text_in, pos_in, text_all, image_all, pos_all, pt_send, pt_all,
-    text_unit, image_unit, td_own, td_send, td_recv, id_acc, id_send, id_recv, id_far, id_far_recv,
+    text_unit, image_unit, td_own, td_acc, td_send, td_recv, id_acc, id_send, id_recv, id_far, id_far_recv,
     coeff_parts, loss_part, loss_recv, ib_all, weight_own, wp_send, wp_recv,
     in_sem, tg_s, tg_f, tg_r, ig_s, ig_r, pg_s, pg_r, pt_s, pt_r, td_s, td_r,
     id_s, id_r, ls_s, ls_r, ib_s, ib_f, ib_d, ib_r, wp_s, wp_r,
@@ -158,8 +158,25 @@
     losses = jnp.zeros((1, QUAD * rows), F32)
 
     def text_dir_copy(i):
-        s = order[i]
-        return remote(td_send.at[s], td_recv.at[z], td_s.at[s], td_r.at[z], dev(s, y, c, x))
+        to = (1 - mid, 1 + mid, 1 + 2 * mid)[i - 1]
+        slot = (0, 2 - mid, 3 - 2 * mid)[i - 1]
+        return remote(td_send.at[i], td_recv.at[slot], td_s.at[i], td_r.at[slot], dev(flip(to), y, c, x))
+
+    def text_dir_wait(slot):
+        remote(td_recv.at[slot], td_recv.at[slot], td_s.at[0], td_r.at[slot], dev(z, y, oc, x)).wait_recv()
+
+    def text_dir_merge(i):
+        @pl.when(mid == 1)
+        def _():
+            text_dir_wait(i)
+            td_send[i] = (td_acc[i - 2] + td_recv[i].astype(F32)).astype(BF16)
+            text_dir_copy(i).start()
+
+    def text_dir_from_end(i):
+        @pl.when(mid == 0)
+        def _():
+            td_send[i] = td_acc[i - 2].astype(BF16)
+            text_dir_copy(i).start()
 
     for i in range(LINE):
         if i == 2:
@@ -186,16 +203,11 @@
         text_part = jnp.dot(coeffs, images, preferred_element_type=F32)
         if i == 0:
             td_own[...] = text_part
+        elif i == 1:
+            td_send[1] = text_part.astype(BF16)
         else:
-            td_send[s] = text_part.astype(BF16)
-        if i == 1:
-
-            @pl.when(mid == 0)
-            def _():
-                text_dir_copy(1).start()
-
-        if i == 2:
-            text_dir_copy(2).start()
+            td_acc[0] = text_part
+            text_dir_from_end(2)
         image_part = lax.dot_general(
             coeffs, text, (((0,), (0,)), ((), ())), preferred_element_type=F32
         ).reshape(QUAD, rows, emb)
@@ -222,16 +234,22 @@
     id_acc[oy * 2 + c] = image_sum(oy, c)
     id_copies[1].wait_recv()
     id_far[...] = (id_acc[oy * 2 + c] + id_recv[1].astype(F32)).astype(BF16)
-    far_copy = remote(id_far, id_far_recv, id_s.at[2], id_r.at[2], dev(z, oy, c, x))
-    far_copy.start()
+    rows_half = rows // 2
+    halves = [pl.ds(0, rows_half), pl.ds(rows_half, rows_half)]
+    far_copies = [
+        remote(id_far.at[h], id_far_recv.at[h], id_s.at[2 + n], id_r.at[2 + n], dev(z, oy, c, x))
+        for n, h in enumerate(halves)
+    ]
+    for copy in far_copies:
+        copy.start()
     near = image_sum(y, c)
-    td_send[s] = jnp.dot(coeffs, images, preferred_element_type=F32).astype(BF16)
+    td_acc[1] = jnp.dot(coeffs, images, preferred_element_type=F32)
+    text_dir_from_end(3)
 
     @pl.when(mid == 1)
     def _():
         text_dir_copy(1).start()
 
-    text_dir_copy(3).start()
     loss_copies = [
         remote(loss_part.at[yy * 2 + cc], loss_recv.at[q], ls_s.at[k], ls_r.at[q], dev(z, yy, cc, x))
         for k, (yy, cc) in enumerate(peers)
@@ -240,26 +258,37 @@
         copy.start()
     id_copies[0].wait_recv()
     near += id_recv[0].astype(F32)
-    far_copy.wait_recv()
-    image_dir = near + id_far_recv[...].astype(F32)
-    unit = image_unit[...]
-    image_back = (
-        (image_dir - unit * jnp.sum(unit * image_dir, axis=-1, keepdims=True)) * image_inv
-    ).astype(BF16)
+
     part = emb // PARTS
-    for k in range(PARTS):
-        ib_all[k, me] = image_back[:, k * part : (k + 1) * part]
-
-    def ib_copy(k, slot, send, *to):
+    own, by_y, by_x, diagonal = (y, c, x), (oy, c, x), (y, c, ox), (oy, c, ox)
+    cuts = [(pl.ds(0, PARTS // 2), 0), (pl.ds(PARTS // 2, PARTS // 2), 0)]
+    cuts += [(pl.ds(k, 1), 1) for k in range(PARTS)]
+
+    def ib_copy(m, slot, send, *to):
+        columns, n = cuts[m]
         j = layer_of(*slot)
-        return remote(ib_all.at[k, j], ib_all.at[k, j], send, ib_r.at[k, j], dev(z, *to))
-
-    own, pair, by_y, by_x, diagonal = (y, c, x), (y, oc, x), (oy, c, x), (y, c, ox), (oy, c, ox)
-    ib_copies = [
-        ib_copy(k, own, ib_s.at[k, n], *to) for k in range(PARTS) for n, to in enumerate((by_x, by_y, pair))
-    ]
-    for copy in ib_copies:
-        copy.start()
+        ref = ib_all.at[columns, j, halves[n]]
+        return remote(ref, ref, send, ib_r.at[m, j], dev(z, *to))
+
+    text_dir_merge(2)
+    ib_copies = []
+    for n in range(2):
+        far_copies[n].wait_recv()
+        lines = slice(n * rows_half, (n + 1) * rows_half)
+        image_dir = near[lines] + id_far_recv[halves[n]].astype(F32)
+        unit = image_unit[halves[n]]
+        image_back = (
+            (image_dir - unit * jnp.sum(unit * image_dir, axis=-1, keepdims=True)) * image_inv[lines]
+        ).astype(BF16)
+        for k in range(PARTS):
+            ib_all[k, me, halves[n]] = image_back[:, k * part : (k + 1) * part]
+        for m, cut in enumerate(cuts):
+            if cut[1] != n:
+                continue
+            for to_n, to in enumerate((by_x, by_y, (y, oc, x))):
+                copy = ib_copy(m, own, ib_s.at[m, to_n], *to)
+                copy.start()
+                ib_copies.append(copy)
 
     def pt_recv(k):
         j = (me + k) % LAYER
@@ -268,6 +297,12 @@
     for k in range(1, LAYER):
         pt_recv(k).wait_recv()
 
+    text_dir_merge(3)
+
+    @pl.when(mid == 0)
+    def _():
+        text_dir_copy(1).start()
+
     share = pt_all.shape[2]
     turned_all = jnp.concatenate([pt_all[j].reshape(LINE * share, rows) for j in range(LAYER)], axis=1)
 
@@ -275,29 +310,33 @@
         t = (z + n) % LINE
         return remote(wp_send.at[k, t], wp_recv.at[k, z], wp_s.at[k, t], wp_r.at[k, z], dev(t, y, c, x))
 
-    for step in range(PARTS + 2):
-        k = step
-        if k < PARTS:
+    pair = (y, oc, x)
+    for step in range(len(cuts) + 2):
+        m = step
+        if m < len(cuts):
             for n, slot in enumerate((by_x, by_y)):
-                ib_copy(k, slot, ib_f.at[k, n], *pair).wait_recv()
-                if k % 2 == n:
-                    on = ib_copy(k, slot, ib_d.at[k], *(by_y if n == 0 else by_x))
+                ib_copy(m, slot, ib_f.at[m, n], *pair).wait_recv()
+                if m % 2 == n:
+                    on = ib_copy(m, slot, ib_d.at[m], *(by_y if n == 0 else by_x))
                     on.start()
                     ib_copies.append(on)
-                on = ib_copy(k, slot, ib_f.at[k, n], *pair)
+                on = ib_copy(m, slot, ib_f.at[m, n], *pair)
                 on.start()
                 ib_copies.append(on)
-        k = step - 1
-        if 0 <= k < PARTS:
-            on = ib_copy(k, diagonal, ib_f.at[k, 2], *pair)
+        m = step - 1
+        if 0 <= m < len(cuts):
+            on = ib_copy(m, diagonal, ib_f.at[m, 2], *pair)
             on.wait_recv()
             on.start()
             ib_copies.append(on)
-        k = step - 2
+        m = step - 2
+        if m < 0:
+            continue
+        for slot in ((y, oc, x), (oy, oc, x), (y, oc, ox), (oy, oc, ox)):
+            ib_copy(m, slot, ib_f.at[m, 0], *pair).wait_recv()
+        k = m - 2
         if k < 0:
             continue
-        for slot in ((y, oc, x), (oy, oc, x), (y, oc, ox), (oy, oc, ox)):
-            ib_copy(k, slot, ib_f.at[k, 0], *pair).wait_recv()
         product = jnp.dot(turned_all, ib_all[k].reshape(LAYER * rows, part), preferred_element_type=F32)
         for t in range(LINE):
             weight_own[k, t] = product[t * share : (t + 1) * share]
@@ -305,11 +344,9 @@
         for n in range(1, LINE):
             weight_copy(k, n).start()
 
-    total = td_own[...]
-    for k in range(1, LINE):
-        t = (z + k) % LINE
-        remote(td_recv.at[t], td_recv.at[t], td_s.at[t], td_r.at[t], dev(t, y, c, x)).wait_recv()
-        total += td_recv[t].astype(F32)
+    text_dir_wait(0)
+    text_dir_wait(1)
+    total = td_own[...] + td_recv[0].astype(F32) + td_recv[1].astype(F32)
     unit = text_unit[...]
     text_out[...] = (total - unit * jnp.sum(unit * total, axis=-1, keepdims=True)) * text_inv
 
@@ -337,7 +374,7 @@
         for i in range(1, LINE):
             forward(i).wait_send()
 
-    for copy in pos_copies + image_copies + [image_pass] + id_copies + [far_copy] + loss_copies:
+    for copy in pos_copies + image_copies + [image_pass] + id_copies + far_copies + loss_copies:
         copy.wait_send()
     for copy in ib_copies:
         copy.wait_send()
@@ -347,6 +384,23 @@
         text_dir_copy(k).wait_send()
         for part in range(PARTS):
             weight_copy(part, k).wait_send()
+
+
+def settle_kernel(loss_in, weight_in, text_in, loss_out, weight_out, text_out):
+    loss_out[...] = loss_in[...]
+    weight_out[...] = weight_in[...]
+    text_out[...] = text_in[...]
+
+
+def settle(*results):
+    in_vmem = pl.BlockSpec(memory_space=pltpu.VMEM)
+    return pl.pallas_call(
+        settle_kernel,
+        out_shape=tuple(jax.ShapeDtypeStruct(r.shape, r.dtype) for r in results),
+        in_specs=[in_vmem] * len(results),
+        out_specs=(in_vmem,) * len(results),
+        compiler_params=pltpu.CompilerParams(vmem_limit_bytes=61 * 2**20),
+    )(*results)
 
 
 def fused(pooled, w_img, text_emb, pos_index, log_scale, bias):
@@ -380,6 +434,7 @@
             vmem(block, F32),
             vmem(block, F32),
             vmem(block, F32),
+            vmem((2,) + block, F32),
             vmem((LINE,) + block, BF16),
             vmem((LINE,) + block, BF16),
             vmem((QUAD,) + block, F32),
@@ -400,15 +455,16 @@
             dma((3,)), dma((QUAD,)),
             dma((LAYER,)), dma((LAYER,)),
             dma((LINE,)), dma((LINE,)),
-            dma((3,)), dma((3,)),
+            dma((4,)), dma((4,)),
             dma((3,)), dma((QUAD,)),
-            dma((PARTS, 3)), dma((PARTS, 3)), dma((PARTS,)), dma((PARTS, LAYER)),
+            dma((PARTS + 2, 3)), dma((PARTS + 2, 3)), dma((PARTS + 2,)), dma((PARTS + 2, LAYER)),
             dma((PARTS, LINE)), dma((PARTS, LINE)),
         ],
         compiler_params=pltpu.CompilerParams(
             collective_id=0, has_side_effects=True, vmem_limit_bytes=63 * 2**20
         ),
     )(pooled[0], w_img, text_emb[0], pos_index, log_scale, bias)
+    loss, weight, text = settle(loss, weight, text)
     return loss, weight, text[None]
 
 

time: 66.2 us -> 63.8 us (0.964)
  local copies, waits for them, and re-layouts: 4.62 us -> 0 us
  Pallas kernels: 59.5 us -> 61.7 us
    unnamed x3 -> x0, local copies, waits for them, and re-layouts: 4.62 us -> none
    pallas_call x0 -> x1, Pallas kernels: none -> 2.03 us  [settle(): pl.pallas_call(settle_kernel, out_shape=tuple((jax.ShapeDtypeStruct(r.sha...]
where the time goes in v5:
time: 63.8 us; the launch traced here: 63.6 us
  Pallas kernels  61.7 us (97%)
  between operations  1.93 us (3%)
    pallas_call x1, Pallas kernels, fused(): pl.pallas_call(fused_kernel, out_shape=(jax.ShapeDtypeStruct((1, rows), F...  59.7 us
    pallas_call x1, Pallas kernels, settle(): pl.pallas_call(settle_kernel, out_shape=tuple((jax.ShapeDtypeStruct(r.sha...  2.03 us

profile of v5, /device:TPU:0, one launch (start us, length us, event | category | flops | bytes accessed | tf_op | source)
XLA Modules:
  0.0 63.6 jit_solution(21363232534814027)
XLA Ops:
  1.9 59.7 %shard_map.85 = (f32[1,128]{1,0:T(1,128)}, f32[48,1024]{1,0:T(8,128)}, f32[128,1024]{1,0:T(8,128)}) custom-call(bf16[128,1536]{1,0:T(8,128)(2,1)} %bitcast.3, bf16[1536,1024]{1,0:T(8,128)(2,1)} %w_hbm.1, bf16[128,1024]{1,0:T(8,128)(2,1)} %bitcast.4, s32[1,128]{1,0:T(1,128)} %pos_hbm.1, f32[1]{0:T(128)S(6)} %copy.9.log_scale, f32[1]{0:T(128)S(6)} %copy.10.bias), custom_call_target="tpu_custom_call" | custom-call | tf_op jit(solution)/shard_map/pallas_call | solution.py:415
  61.6 2.0 %shard_map.86 = (f32[1,128]{1,0:T(1,128)}, f32[48,1024]{1,0:T(8,128)}, f32[128,1024]{1,0:T(8,128)}) custom-call(f32[1,128]{1,0:T(1,128)} %get-tuple-element.9.loss_in, f32[48,1024]{1,0:T(8,128)} %get-tuple-element.10.weight_in, f32[128,1024]{1,0:T(8,128)} %get-tuple-element.11.text_in), custom_call_target="tpu_custom_call" | custom-call | tf_op jit(solution)/shard_map/pallas_call | solution.py:397

commit v6 on v5

--- a/solution.py
+++ b/solution.py
@@ -20,7 +20,7 @@
     text_unit, image_unit, td_own, td_acc, td_send, td_recv, id_acc, id_send, id_recv, id_far, id_far_recv,
     coeff_parts, loss_part, loss_recv, ib_all, weight_own, wp_send, wp_recv,
     in_sem, tg_s, tg_f, tg_r, ig_s, ig_r, pg_s, pg_r, pt_s, pt_r, td_s, td_r,
-    id_s, id_r, ls_s, ls_r, ib_s, ib_f, ib_d, ib_r, wp_s, wp_r,
+    id_s, id_r, ls_s, ls_r, ib_s, ib_d, ib_r, wp_s, wp_r,
 ):
     blk, x = lax.axis_index("blk"), lax.axis_index("rep")
     z, y, c = blk // 4, (blk // 2) % 2, blk % 2
@@ -59,9 +59,10 @@
     for k in range(1, LAYER):
         pl.semaphore_signal(barrier, inc=1, device_id=layer_dev((me + k) % LAYER), device_id_type=pl.DeviceIdType.MESH)
     for k in range(1, LINE):
-        pl.semaphore_signal(
-            barrier, inc=1, device_id=dev((z + k) % LINE, y, c, x), device_id_type=pl.DeviceIdType.MESH
-        )
+        for cc in (c, oc):
+            pl.semaphore_signal(
+                barrier, inc=1, device_id=dev((z + k) % LINE, y, cc, x), device_id_type=pl.DeviceIdType.MESH
+            )
 
     ins[0].wait()
     raw = text_in[...].astype(F32)
@@ -71,7 +72,7 @@
     text_all[z] = unit.astype(BF16)
     ins[1].wait()
     pos_all[q] = pos_in[...]
-    pl.semaphore_wait(barrier, LAYER - 1 + LINE - 1)
+    pl.semaphore_wait(barrier, LAYER - 1 + 2 * (LINE - 1))
 
     own_a = remote(text_all.at[z], text_all.at[z], tg_s.at[0], tg_r.at[z], dev(flip(1 + mid), y, c, x))
     own_b = remote(text_all.at[z], text_all.at[z], tg_s.at[1], tg_r.at[z], dev(flip(0), y, c, x))
@@ -106,12 +107,13 @@
     turned = pooled[...].T.reshape(LINE, LAYER, -1, rows)
     for j in range(LAYER):
         for t in range(LINE):
-            pt_send[j, t] = turned[t, j]
-    pt_all[me] = pt_send[me]
+            pt_send[j // 4, j % 2, (j // 2) % 2, t] = turned[t, j]
+    pt_all[y, x] = pt_send[y, x]
+    same_core = [(oy, x), (y, ox), (oy, ox)]
 
     def pt_copy(k):
-        j = (me + k) % LAYER
-        return remote(pt_send.at[j], pt_all.at[me], pt_s.at[j], pt_r.at[me], layer_dev(j))
+        to = same_core[k]
+        return remote(pt_send.at[to], pt_all.at[y, x], pt_s.at[k], pt_r.at[y, x], dev(z, to[0], c, to[1]))
 
     def forward(i):
         s = order[i]
@@ -148,7 +150,7 @@
     image_slot(0, y, oc).wait_recv()
     image_slot(0, oy, oc).wait_recv()
 
-    for k in range(1, LAYER):
+    for k in range(3):
         pt_copy(k).start()
 
     images = image_all[...].reshape(QUAD * rows, emb)
@@ -266,7 +268,7 @@
 
     def ib_copy(m, slot, send, *to):
         columns, n = cuts[m]
-        j = layer_of(*slot)
+        j = slot[0] * 2 + slot[2]
         ref = ib_all.at[columns, j, halves[n]]
         return remote(ref, ref, send, ib_r.at[m, j], dev(z, *to))
 
@@ -281,21 +283,17 @@
             (image_dir - unit * jnp.sum(unit * image_dir, axis=-1, keepdims=True)) * image_inv[lines]
         ).astype(BF16)
         for k in range(PARTS):
-            ib_all[k, me, halves[n]] = image_back[:, k * part : (k + 1) * part]
+            ib_all[k, y * 2 + x, halves[n]] = image_back[:, k * part : (k + 1) * part]
         for m, cut in enumerate(cuts):
             if cut[1] != n:
                 continue
-            for to_n, to in enumerate((by_x, by_y, (y, oc, x))):
+            for to_n, to in enumerate((by_x, by_y)):
                 copy = ib_copy(m, own, ib_s.at[m, to_n], *to)
                 copy.start()
                 ib_copies.append(copy)
 
-    def pt_recv(k):
-        j = (me + k) % LAYER
-        return remote(pt_all.at[j], pt_all.at[j], pt_s.at[j], pt_r.at[j], layer_dev(j))
-
-    for k in range(1, LAYER):
-        pt_recv(k).wait_recv()
+    for k, slot in enumerate(same_core):
+        remote(pt_all.at[slot], pt_all.at[slot], pt_s.at[k], pt_r.at[slot], dev(z, slot[0], c, slot[1])).wait_recv()
 
     text_dir_merge(3)
 
@@ -303,45 +301,38 @@
     def _():
         text_dir_copy(1).start()
 
-    share = pt_all.shape[2]
-    turned_all = jnp.concatenate([pt_all[j].reshape(LINE * share, rows) for j in range(LAYER)], axis=1)
+    share = pt_all.shape[4]
+    turned_all = jnp.concatenate(
+        [pt_all[j // 2, j % 2].reshape(LAYER * share, rows) for j in range(QUAD)], axis=1
+    )
+    line = [(cc, (z + n) % LINE) for n in range(LINE) for cc in (c, oc)][1:]
 
     def weight_copy(k, n):
-        t = (z + n) % LINE
-        return remote(wp_send.at[k, t], wp_recv.at[k, z], wp_s.at[k, t], wp_r.at[k, z], dev(t, y, c, x))
-
-    pair = (y, oc, x)
-    for step in range(len(cuts) + 2):
+        cc, t = line[n]
+        return remote(wp_send.at[k, cc, t], wp_recv.at[k, c, z], wp_s.at[k, n], wp_r.at[k, c, z], dev(t, y, cc, x))
+
+    for step in range(len(cuts) + 1):
         m = step
         if m < len(cuts):
             for n, slot in enumerate((by_x, by_y)):
-                ib_copy(m, slot, ib_f.at[m, n], *pair).wait_recv()
+                to = by_y if n == 0 else by_x
+                on = ib_copy(m, slot, ib_d.at[m], *to)
+                on.wait_recv()
                 if m % 2 == n:
-                    on = ib_copy(m, slot, ib_d.at[m], *(by_y if n == 0 else by_x))
                     on.start()
                     ib_copies.append(on)
-                on = ib_copy(m, slot, ib_f.at[m, n], *pair)
-                on.start()
-                ib_copies.append(on)
         m = step - 1
-        if 0 <= m < len(cuts):
-            on = ib_copy(m, diagonal, ib_f.at[m, 2], *pair)
-            on.wait_recv()
-            on.start()
-            ib_copies.append(on)
-        m = step - 2
         if m < 0:
             continue
-        for slot in ((y, oc, x), (oy, oc, x), (y, oc, ox), (oy, oc, ox)):
-            ib_copy(m, slot, ib_f.at[m, 0], *pair).wait_recv()
+        ib_copy(m, diagonal, ib_d.at[m], *by_y).wait_recv()
         k = m - 2
         if k < 0:
             continue
-        product = jnp.dot(turned_all, ib_all[k].reshape(LAYER * rows, part), preferred_element_type=F32)
-        for t in range(LINE):
-            weight_own[k, t] = product[t * share : (t + 1) * share]
-            wp_send[k, t] = product[t * share : (t + 1) * share].astype(BF16)
-        for n in range(1, LINE):
+        product = jnp.dot(turned_all, ib_all[k].reshape(QUAD * rows, part), preferred_element_type=F32)
+        product = product.reshape(2, LINE, share, part)
+        weight_own[k] = product
+        wp_send[k] = product.astype(BF16)
+        for n in range(len(line)):
             weight_copy(k, n).start()
 
     text_dir_wait(0)
@@ -358,12 +349,11 @@
     loss_out[...] = total / (LINE * QUAD * rows)
 
     for k in range(PARTS):
-        total = weight_own[k, z]
-        for n in range(1, LINE):
-            t = (z + n) % LINE
-            slot = wp_recv.at[k, t]
-            remote(slot, slot, wp_s.at[k, t], wp_r.at[k, t], dev(t, y, c, x)).wait_recv()
-            total += wp_recv[k, t].astype(F32)
+        total = weight_own[k, c, z]
+        for n, (cc, t) in enumerate(line):
+            slot = wp_recv.at[k, cc, t]
+            remote(slot, slot, wp_s.at[k, n], wp_r.at[k, cc, t], dev(t, y, cc, x)).wait_recv()
+            total += wp_recv[k, cc, t].astype(F32)
         weight_out[:, k * part : (k + 1) * part] = total / 64.0
 
     own_a.wait_send()
@@ -378,12 +368,12 @@
         copy.wait_send()
     for copy in ib_copies:
         copy.wait_send()
-    for k in range(1, LAYER):
+    for k in range(3):
         pt_copy(k).wait_send()
-    for k in range(1, LINE):
-        text_dir_copy(k).wait_send()
-        for part in range(PARTS):
-            weight_copy(part, k).wait_send()
+        text_dir_copy(k + 1).wait_send()
+    for part in range(PARTS):
+        for n in range(len(line)):
+            weight_copy(part, n).wait_send()
 
 
 def settle_kernel(loss_in, weight_in, text_in, loss_out, weight_out, text_out):
@@ -429,8 +419,8 @@
             vmem((LINE,) + block, BF16),
             vmem((QUAD,) + block, BF16),
             vmem((QUAD, 1, rows), jnp.int32),
-            vmem((LAYER, LINE, share, rows), BF16),
-            vmem((LAYER, LINE, share, rows), BF16),
+            vmem((2, 2, 2, LINE, share, rows), BF16),
+            vmem((2, 2, 2, LINE, share, rows), BF16),
             vmem(block, F32),
             vmem(block, F32),
             vmem(block, F32),
@@ -445,20 +435,20 @@
             vmem((QUAD, rows, rows), BF16),
             vmem((QUAD, 1, rows), F32),
             vmem((QUAD, 1, rows), F32),
-            vmem((PARTS, LAYER, rows, emb // PARTS), BF16),
-            vmem((PARTS, LINE, share, emb // PARTS), F32),
-            vmem((PARTS, LINE, share, emb // PARTS), BF16),
-            vmem((PARTS, LINE, share, emb // PARTS), BF16),
+            vmem((PARTS, QUAD, rows, emb // PARTS), BF16),
+            vmem((PARTS, 2, LINE, share, emb // PARTS), F32),
+            vmem((PARTS, 2, LINE, share, emb // PARTS), BF16),
+            vmem((PARTS, 2, LINE, share, emb // PARTS), BF16),
             dma((4,)),
             dma((2,)), dma((LINE,)), dma((LINE,)),
             dma((3,)), dma((QUAD,)),
             dma((3,)), dma((QUAD,)),
-            dma((LAYER,)), dma((LAYER,)),
+            dma((3,)), dma((2, 2)),
             dma((LINE,)), dma((LINE,)),
             dma((4,)), dma((4,)),
             dma((3,)), dma((QUAD,)),
-            dma((PARTS + 2, 3)), dma((PARTS + 2, 3)), dma((PARTS + 2,)), dma((PARTS + 2, LAYER)),
-            dma((PARTS, LINE)), dma((PARTS, LINE)),
+            dma((PARTS + 2, 2)), dma((PARTS + 2,)), dma((PARTS + 2, QUAD)),
+            dma((PARTS, LAYER)), dma((PARTS, 2, LINE)),
         ],
         compiler_params=pltpu.CompilerParams(
             collective_id=0, has_side_effects=True, vmem_limit_bytes=63 * 2**20

time: 63.8 us -> 68.2 us (1.069)
  Pallas kernels: 61.7 us -> 66.1 us
    pallas_call x1, Pallas kernels: 59.7 us -> 64 us  [fused(): pl.pallas_call(fused_kernel, out_shape=(jax.ShapeDtypeStruct((1, rows), F...]
where the time goes in v6:
time: 68.2 us; the launch traced here: 68 us
  Pallas kernels  66.1 us (97%)
  between operations  1.93 us (3%)
    pallas_call x1, Pallas kernels, fused(): pl.pallas_call(fused_kernel, out_shape=(jax.ShapeDtypeStruct((1, rows), F...  64 us
    pallas_call x1, Pallas kernels, settle(): pl.pallas_call(settle_kernel, out_shape=tuple((jax.ShapeDtypeStruct(r.sha...  2.03 us

profile of v6, /device:TPU:0, one launch (start us, length us, event | category | flops | bytes accessed | tf_op | source)
XLA Modules:
  0.0 68.0 jit_solution(18174145594305329818)
XLA Ops:
  1.9 64.0 %shard_map.85 = (f32[1,128]{1,0:T(1,128)}, f32[48,1024]{1,0:T(8,128)}, f32[128,1024]{1,0:T(8,128)}) custom-call(bf16[128,1536]{1,0:T(8,128)(2,1)} %bitcast.3, bf16[1536,1024]{1,0:T(8,128)(2,1)} %w_hbm.1, bf16[128,1024]{1,0:T(8,128)(2,1)} %bitcast.4, s32[1,128]{1,0:T(1,128)} %pos_hbm.1, f32[1]{0:T(128)S(6)} %copy.9.log_scale, f32[1]{0:T(128)S(6)} %copy.10.bias), custom_call_target="tpu_custom_call" | custom-call | tf_op jit(solution)/shard_map/pallas_call | solution.py:405
  66.0 2.0 %shard_map.86 = (f32[1,128]{1,0:T(1,128)}, f32[48,1024]{1,0:T(8,128)}, f32[128,1024]{1,0:T(8,128)}) custom-call(f32[1,128]{1,0:T(1,128)} %get-tuple-element.9.loss_in, f32[48,1024]{1,0:T(8,128)} %get-tuple-element.10.weight_in, f32[128,1024]{1,0:T(8,128)} %get-tuple-element.11.text_in), custom_call_target="tpu_custom_call" | custom-call | tf_op jit(solution)/shard_map/pallas_call | solution.py:387

commit v7 on v5

--- a/solution.py
+++ b/solution.py
@@ -297,8 +297,6 @@
     for k in range(1, LAYER):
         pt_recv(k).wait_recv()
 
-    text_dir_merge(3)
-
     @pl.when(mid == 0)
     def _():
         text_dir_copy(1).start()
@@ -323,6 +321,8 @@
                 on = ib_copy(m, slot, ib_f.at[m, n], *pair)
                 on.start()
                 ib_copies.append(on)
+        if m == 1:
+            text_dir_merge(3)
         m = step - 1
         if 0 <= m < len(cuts):
             on = ib_copy(m, diagonal, ib_f.at[m, 2], *pair)

time: 63.8 us -> 63.8 us (level)
  no operation moved by 1% of the time
where the time goes in v7:
time: 63.8 us; the launch traced here: 63.6 us
  Pallas kernels  61.7 us (97%)
  between operations  1.93 us (3%)
    pallas_call x1, Pallas kernels, fused(): pl.pallas_call(fused_kernel, out_shape=(jax.ShapeDtypeStruct((1, rows), F...  59.7 us
    pallas_call x1, Pallas kernels, settle(): pl.pallas_call(settle_kernel, out_shape=tuple((jax.ShapeDtypeStruct(r.sha...  2.03 us

profile of v7, /device:TPU:0, one launch (start us, length us, event | category | flops | bytes accessed | tf_op | source)
XLA Modules:
  0.0 63.6 jit_solution(5671701980193292804)
XLA Ops:
  1.9 59.7 %shard_map.85 = (f32[1,128]{1,0:T(1,128)}, f32[48,1024]{1,0:T(8,128)}, f32[128,1024]{1,0:T(8,128)}) custom-call(bf16[128,1536]{1,0:T(8,128)(2,1)} %bitcast.3, bf16[1536,1024]{1,0:T(8,128)(2,1)} %w_hbm.1, bf16[128,1024]{1,0:T(8,128)(2,1)} %bitcast.4, s32[1,128]{1,0:T(1,128)} %pos_hbm.1, f32[1]{0:T(128)S(6)} %copy.9.log_scale, f32[1]{0:T(128)S(6)} %copy.10.bias), custom_call_target="tpu_custom_call" | custom-call | tf_op jit(solution)/shard_map/pallas_call | solution.py:415
  61.6 2.0 %shard_map.86 = (f32[1,128]{1,0:T(1,128)}, f32[48,1024]{1,0:T(8,128)}, f32[128,1024]{1,0:T(8,128)}) custom-call(f32[1,128]{1,0:T(1,128)} %get-tuple-element.9.loss_in, f32[48,1024]{1,0:T(8,128)} %get-tuple-element.10.weight_in, f32[128,1024]{1,0:T(8,128)} %get-tuple-element.11.text_in), custom_call_target="tpu_custom_call" | custom-call | tf_op jit(solution)/shard_map/pallas_call | solution.py:397
